TPU v7x, 32 devices: a whole 2x2x4 slice. The times are simulated.
32 devices in a mesh: dp: 8 (over y, x, core), swap: 4 (over z).
Axes of the slice: x: 2, y: 2, z: 4, core: 2. Of those that a mesh axis runs over, the one named last changes fastest.
Arguments:
- source_tiles_smallest: bfloat16 [100, 192, 384], P(None, 'dp', 'swap'), may hold values from -6 to 6
- source_tiles_moderate: bfloat16 [196, 192, 384], P(None, 'dp', 'swap'), may hold values from -6 to 6
- source_tiles_largest: bfloat16 [324, 64, 384], P(None, 'dp', 'swap'), may hold values from -6 to 6
- target_cotangent_smallest: bfloat16 [100, 192, 384], P(None, 'dp', 'swap'), may hold values from -6 to 6
- target_cotangent_moderate: bfloat16 [196, 192, 384], P(None, 'dp', 'swap'), may hold values from -6 to 6
- target_cotangent_largest: bfloat16 [324, 64, 384], P(None, 'dp', 'swap'), may hold values from -6 to 6
- surviving_tallies: int32 [8, 3], P('dp'), may hold values from 4 to 24, as said below
- token_affine_factor: float32 [2, 384], replicated, may hold values from 0.1 to 1.9
- token_affine_addend: float32 [2, 384], replicated, may hold values from -1.75 to 1.75
- crosstile_matrix_smallest: bfloat16 [2, 100, 100], replicated, may hold values from -0.625 to 0.625
- crosstile_matrix_moderate: bfloat16 [2, 196, 196], replicated, may hold values from -0.4375 to 0.4375
- crosstile_matrix_largest: bfloat16 [2, 324, 324], replicated, may hold values from -0.3125 to 0.3125
- crosstile_addend_smallest: float32 [2, 100], replicated, may hold values from -1.75 to 1.75
- crosstile_addend_moderate: float32 [2, 196], replicated, may hold values from -1.75 to 1.75
- crosstile_addend_largest: float32 [2, 324], replicated, may hold values from -1.75 to 1.75
- token_blend_factor: float32 [2, 384], replicated, may hold values from 0.3 to 1
- feedforward_affine_factor: float32 [2, 384], replicated, may hold values from 0.1 to 1.9
- feedforward_affine_addend: float32 [2, 384], replicated, may hold values from -1.75 to 1.75
- widening_matrix: bfloat16 [2, 384, 1536], replicated, may hold values from -0.3125 to 0.3125
- widening_addend: float32 [2, 1536], replicated, may hold values from -1.75 to 1.75
- narrowing_matrix: bfloat16 [2, 1536, 384], replicated, may hold values from -0.15625 to 0.15625
- narrowing_addend: float32 [2, 384], replicated, may hold values from -1.75 to 1.75
- feedforward_factor: float32 [2, 384], replicated, may hold values from 0.3 to 1
Outputs:
- out_small: float32 [100, 192, 384], P(None, 'dp', 'swap')
- out_medium: float32 [196, 192, 384], P(None, 'dp', 'swap')
- out_large: float32 [324, 64, 384], P(None, 'dp', 'swap')
- grad_small: float32 [100, 192, 384], P(None, 'dp', 'swap')
- grad_medium: float32 [196, 192, 384], P(None, 'dp', 'swap')
- grad_large: float32 [324, 64, 384], P(None, 'dp', 'swap')
- grad_prescale: float32 [2, 384], replicated
- grad_preshift: float32 [2, 384], replicated
- grad_mix_small: float32 [2, 100, 100], replicated
- grad_mix_medium: float32 [2, 196, 196], replicated
- grad_mix_large: float32 [2, 324, 324], replicated
- grad_bias_small: float32 [2, 100], replicated
- grad_bias_medium: float32 [2, 196], replicated
- grad_bias_large: float32 [2, 324], replicated
- grad_mixgain: float32 [2, 384], replicated
- grad_mlpscale: float32 [2, 384], replicated
- grad_mlpshift: float32 [2, 384], replicated
- grad_weight_in: float32 [2, 384, 1536], replicated
- grad_bias_in: float32 [2, 1536], replicated
- grad_weight_out: float32 [2, 1536, 384], replicated
- grad_bias_out: float32 [2, 384], replicated
- grad_mlpgain: float32 [2, 384], replicated
Inputs may be any that keep to these rules, and one draw needn't show every extreme that they name: surviving_tallies[i, g] is the number of live images of group g on index i of dp, which occupy that index's first slots; at least half of its 24, 24 or 8 slots are live, and in every group some index is full.
All inputs are finite; a program needn't handle non-finite values.
Results may differ from a plain program's by a relative error of at most 0.01.
Values may be sent and summed in bfloat16 or wider, within the bound.
No kernel may reach another device: no remote copies, remote signals or barrier semaphores. Data moves between devices by JAX's collectives and lax.ppermute only.
A program may use at most 192 MiB of HBM per device.

v0:
```python
import functools

import jax
import jax.numpy as jnp
from jax import lax
from jax.experimental import pallas as pl
from jax.experimental.layout import Layout, with_layout_constraint
from jax.experimental.pallas import tpu as pltpu
from jax.sharding import PartitionSpec as P

BF = jnp.bfloat16
F32 = jnp.float32
FFC = 256
ROWS = 384
VMEM_LIMIT = 64 << 20


def round_up(value, unit):
    return -(-value // unit) * unit


def nt(a, b):
    return lax.dot_general(a, b, (((1,), (1,)), ((), ())), preferred_element_type=F32)


def tn(a, b):
    return lax.dot_general(a, b, (((0,), (0,)), ((), ())), preferred_element_type=F32)


def nn(a, b):
    return jnp.dot(a, b, preferred_element_type=F32)


class Piece:
    def __init__(self, members, patches):
        self.members = []
        offset = 0
        for group, index in members:
            self.members.append((group, index, offset))
            offset += patches[group]
        self.total = offset
        self.width = round_up(offset, 128)
        self.work = round_up(offset, 128)
        self.groups = sorted({group for group, _ in members})


def pack_kernel(piece, k, patches, masked, me_ref, live_ref, *refs):
    ng = len(piece.groups)
    xs = dict(zip(piece.groups, refs[:ng]))
    outs = refs[ng:]
    me = me_ref[0]
    for s in range(k):
        owner = lax.rem(me + s, k)
        out = outs[s]
        for group, index, offset in piece.members:
            p = patches[group]
            image = owner + k * index
            v = xs[group][image]
            if masked:
                v = (v.astype(F32) * (image < live_ref[group]).astype(F32)).astype(BF)
            out[:, offset : offset + p] = v
        if piece.width > piece.total:
            out[:, piece.total :] = jnp.zeros((out.shape[0], piece.width - piece.total), BF)


def pack(piece, k, patches, me, live, tensors, masked):
    c = tensors[0].shape[1]
    vmem = pl.BlockSpec(memory_space=pltpu.VMEM)
    smem = pl.BlockSpec(memory_space=pltpu.SMEM)
    return pl.pallas_call(
        functools.partial(pack_kernel, piece, k, patches, masked),
        out_shape=[jax.ShapeDtypeStruct((c, piece.width), BF)] * k,
        in_specs=[smem, smem] + [vmem] * len(piece.groups),
        out_specs=[vmem] * k,
        compiler_params=pltpu.CompilerParams(vmem_limit_bytes=32 << 20),
        name="pack",
    )(me, live, *[tensors[g] for g in piece.groups])


def unpack_kernel(pieces, groups, k, patches, masked, me_ref, live_ref, *refs):
    buffers = [refs[i * k : (i + 1) * k] for i in range(len(pieces))]
    outs = refs[len(pieces) * k :]
    me = me_ref[0]
    for piece, bufs in zip(pieces, buffers):
        for s in range(k):
            owner = lax.rem(me - s + k, k)
            for group, index, offset in piece.members:
                if group not in groups:
                    continue
                p = patches[group]
                image = owner + k * index
                v = bufs[s][:, offset : offset + p].astype(F32)
                if masked:
                    v = v * (image < live_ref[group]).astype(F32)
                outs[groups.index(group)][image] = v


def unpack(pieces, groups, k, patches, images, me, live, buffers, masked):
    c = buffers[0][0].shape[0]
    vmem = pl.BlockSpec(memory_space=pltpu.VMEM)
    smem = pl.BlockSpec(memory_space=pltpu.SMEM)
    return pl.pallas_call(
        functools.partial(unpack_kernel, pieces, groups, k, patches, masked),
        out_shape=[jax.ShapeDtypeStruct((images[g], c, patches[g]), F32) for g in groups],
        in_specs=[smem, smem] + [vmem] * (k * len(pieces)),
        out_specs=[vmem] * len(groups),
        compiler_params=pltpu.CompilerParams(vmem_limit_bytes=32 << 20),
        name="unpack",
    )(me, live, *[b for bufs in buffers for b in bufs])


class Rows:
    def __init__(self, ff, width, patches, blocks):
        self.out = ff
        base = 2 * ff
        self.mix = [
            (base + round_up(patches[2], 8), round_up(patches[1], 128)),
            (base + round_up(patches[2], 8), 0),
            (base, 0),
        ]
        self.misc = base
        base += round_up(patches[2], 8) + round_up(patches[1], 8)
        self.bias_in = base
        self.patch = [base + ff // width + g for g in range(3)]
        self.vec = round_up(base + ff // width + 3, 8)
        self.used = self.vec + 8
        self.blocks = blocks
        self.block = round_up(-(-self.used // blocks), 8)
        self.total = blocks * self.block


def over_rows(count, body):
    def step(i, carry):
        body(pl.ds(pl.multiple_of(i * ROWS, ROWS), ROWS))
        return carry

    lax.fori_loop(0, count // ROWS, step, 0)


def channel(cols, layer, j):
    return lambda r: cols[layer, r, j : j + 1]


class Copies:
    def __init__(self, sem):
        self.sem, self.count = sem, 0
        self.started = {}

    def start(self, key, src, dst):
        cp = pltpu.make_async_copy(src, dst, self.sem.at[self.count])
        self.count += 1
        cp.start()
        self.started[key] = cp

    def wait(self, *keys):
        for key in keys:
            self.started.pop(key).wait()

    def wait_all(self):
        self.wait(*list(self.started))


KEPT = ("state", "mixs", "nrm", "sc", "brs", "act", "dact")


def kept_shapes(layer, D, F, W):
    return {
        "state": ((D, W), BF if layer == 0 else F32),
        "mixs": ((D, W), F32),
        "nrm": ((D, W), BF),
        "sc": ((D, W), BF),
        "brs": ((D, W), BF),
        "act": ((F, W), BF),
        "dact": ((F, W), BF),
    }


def load_columns(refs, line, cols, layers):
    line[...] = jnp.zeros(line.shape, F32)
    for l in range(layers):
        for j, ref in enumerate(refs):
            line[j : j + 1, :] = ref[l : l + 1, :]
        cols[l] = jnp.transpose(line[...])


def forward_kernel(piece, k, patches, layers, *refs):
    refs = list(refs)

    def take(n):
        out, refs[:] = refs[:n], refs[n:]
        return out

    (me_ref,) = take(1)
    ins = take(k)
    w1_h, w2_h = take(2)
    mix = dict(zip(piece.groups, take(len(piece.groups))))
    bias = dict(zip(piece.groups, take(len(piece.groups))))
    vectors = take(7)
    (b1_ref,) = take(1)
    outs = take(k)
    kept_h = [dict(zip(KEPT, take(len(KEPT)))) for _ in range(layers)]
    kept = [dict(zip(KEPT, take(len(KEPT)))) for _ in range(layers)]
    last, w1, w2, line, cols, sem = refs
    D, W = last.shape
    F = w2.shape[1]
    c = D // k
    me = me_ref[0]
    copies = Copies(sem)
    for l in range(layers):
        copies.start((l, "w1"), w1_h.at[l], w1.at[l, pl.ds(0, D)])
        copies.start((l, "w2"), w2_h.at[l], w2.at[l])

    def keep(l, name):
        copies.start((l, name), kept[l][name].at[pl.ds(0, D)], kept_h[l][name])

    x0 = kept[0]["state"]
    for s in range(k):
        at = pl.ds(pl.multiple_of(lax.rem(me - s + k, k) * c, 16), c)
        x0[at, : piece.width] = ins[s][...]
    if W > piece.width:
        x0[:, piece.width :] = jnp.zeros((D, W - piece.width), BF)
    keep(0, "state")
    load_columns(vectors, line, cols, layers)

    for l in range(layers):
        a, b, g, f, h, ff, b2 = [channel(cols, l, j) for j in range(7)]
        state, mixs, nrm, sc, brs, act, dact = [kept[l][name] for name in KEPT]
        nxt = kept[l + 1]["state"] if l + 1 < layers else last
        if W > piece.total:
            mixs[:, piece.total :] = jnp.zeros((D, W - piece.total), F32)

        def normalise(r):
            nrm[r, :] = (state[r, :].astype(F32) * a(r) + b(r)).astype(BF)

        over_rows(D, normalise)
        keep(l, "nrm")
        for group, _, o in piece.members:
            p = patches[group]
            mixs[:, o : o + p] = nt(nrm[:, o : o + p], mix[group][l]) + bias[group][l : l + 1, :]

        def blend(r):
            middle = state[r, :].astype(F32) + g(r) * mixs[r, :]
            nxt[r, :] = middle
            sc[r, :] = (middle * f(r) + h(r)).astype(BF)

        over_rows(D, blend)
        keep(l, "mixs")
        keep(l, "sc")
        sc[D:, :] = jnp.ones((sc.shape[0] - D, W), BF)
        rest = b1_ref[l : l + 1, :]
        parts = []
        for _ in range(3):
            parts.append(rest.astype(BF).astype(F32))
            rest = rest - parts[-1]
        parts.append(jnp.zeros((w1.shape[1] - D - 3, F), F32))
        w1[l, D:, :] = jnp.concatenate(parts, 0).astype(BF)
        copies.wait((l, "w1"), (l, "w2"))
        s = sc[...]
        for i in range(F // FFC):
            fr = pl.ds(i * FFC, FFC)
            v = tn(w1[l, :, fr], s)
            v2 = v * v
            t = jnp.tanh(v * (0.7978845608 + (0.7978845608 * 0.044715) * v2))
            hp = 0.5 * t + 0.5
            ac = v * hp
            q = 2 * 0.7978845608 + (6 * 0.7978845608 * 0.044715) * v2
            act[fr, :] = ac.astype(BF)
            dact[fr, :] = (hp + (ac - ac * hp) * q).astype(BF)
            for name in ("act", "dact"):
                copies.start((l, name, i), kept[l][name].at[fr], kept_h[l][name].at[fr])
        br = (tn(w2[l], act[...]) + cols[l, :, 6:7]).astype(BF)
        brs[...] = br
        nxt[...] = nxt[...] + cols[l, :, 5:6] * br.astype(F32)
        keep(l, "brs")
        if l + 1 < layers:
            keep(l + 1, "state")

    for s in range(k):
        at = pl.ds(pl.multiple_of(lax.rem(me + s, k) * c, 16), c)
        outs[s][...] = last[at, : piece.width].astype(BF)
    copies.wait_all()


def with_ones(shapes, D, W):
    return {**shapes, "sc": ((D + 16, W), BF)}


def forward(piece, k, patches, me, bufs, w1, w2, mixes, biases, vectors, b1):
    L, D, F = w1.shape
    W = piece.work
    vmem = pl.BlockSpec(memory_space=pltpu.VMEM)
    smem = pl.BlockSpec(memory_space=pltpu.SMEM)
    hbm = pl.BlockSpec(memory_space=pl.ANY)
    args = [me, *bufs, w1, w2, *[mixes[g] for g in piece.groups], *[biases[g] for g in piece.groups], *vectors, b1]
    specs = [smem] + [vmem] * k + [hbm] * 2 + [vmem] * (2 * len(piece.groups) + len(vectors) + 1)
    c = bufs[0].shape[0]
    kept = [shape for l in range(L) for shape in kept_shapes(l, D, F, W).values()]
    scratch = [pltpu.VMEM(*v) for l in range(L) for v in with_ones(kept_shapes(l, D, F, W), D, W).values()]
    scratch += [
        pltpu.VMEM((D, W), F32),
        pltpu.VMEM((L, D + 16, F), BF),
        pltpu.VMEM((L, F, D), BF),
        pltpu.VMEM((128, D), F32),
        pltpu.VMEM((L, D, 128), F32),
        pltpu.SemaphoreType.DMA((L * (7 + 2 * (F // FFC)),)),
    ]
    out = pl.pallas_call(
        functools.partial(forward_kernel, piece, k, patches, L),
        out_shape=[jax.ShapeDtypeStruct((c, piece.width), BF)] * k + [jax.ShapeDtypeStruct(*v) for v in kept],
        in_specs=specs,
        out_specs=[vmem] * k + [hbm] * len(kept),
        scratch_shapes=scratch,
        compiler_params=pltpu.CompilerParams(vmem_limit_bytes=VMEM_LIMIT),
        name="forward",
    )(*args)
    n = len(KEPT)
    return out[:k], out[k:]


def backward_kernel(piece, k, patches, rows, layers, first, final, *refs):
    refs = list(refs)

    def take(n):
        out, refs[:] = refs[:n], refs[n:]
        return out

    (me_ref,) = take(1)
    ins = take(k)
    kept_h = [dict(zip(KEPT, take(len(KEPT)))) for _ in range(layers)]
    w1_h, w2_h = take(2)
    mix = dict(zip(piece.groups, take(len(piece.groups))))
    vectors = take(7)
    accs_h = [] if first else take(layers)
    outs = take(k)
    sums_h = [take(2 if final else 1) for _ in range(layers)]
    kept = [dict(zip(KEPT, take(len(KEPT)))) for _ in range(layers)]
    gn, gb, gs, dy, w1s, w2s, accs, stages, gb1, gcol, gpb, line, cols, sem = refs
    D, W = gn.shape
    F = w2s.shape[1]
    c = D // k
    me = me_ref[0]
    core = lax.rem(me_ref[1], 2)
    copies = Copies(sem)
    half_f = F // 2
    for l in reversed(range(layers)):
        copies.start((l, "brs"), kept_h[l]["brs"], kept[l]["brs"])
        copies.start((l, "w2"), w2_h.at[l], w2s.at[l])
        for i in range(2):
            at = pl.ds(i * half_f, half_f)
            copies.start((l, "dact", i), kept_h[l]["dact"].at[at], kept[l]["dact"].at[at])
        copies.start((l, "w1"), w1_h.at[l], w1s.at[l])
        copies.start((l, "sc"), kept_h[l]["sc"], kept[l]["sc"].at[pl.ds(0, D)])
        if not first:
            copies.start((l, "acc"), accs_h[l], accs.at[l])
        for name in ("act", "mixs", "state", "nrm"):
            copies.start((l, name), kept_h[l][name], kept[l][name])

    load_columns(vectors, line, cols, layers)
    for s in range(k):
        at = pl.ds(pl.multiple_of(lax.rem(me - s + k, k) * c, 16), c)
        dy[at, : piece.width] = ins[s][...].astype(F32)
    if W > piece.width:
        dy[:, piece.width :] = jnp.zeros((D, W - piece.width), F32)
    if W > piece.total:
        gn[:, piece.total :] = jnp.zeros((D, W - piece.total), F32)
    gcol[...] = jnp.zeros(gcol.shape, F32)

    def put(r, j, v):
        gcol[r, j : j + 1] = jnp.sum(v, 1, keepdims=True)

    for l in reversed(range(layers)):
        a, b, g, f, h, ff, b2 = [channel(cols, l, j) for j in range(7)]
        state, mixs, nrm, sc, brs, act, dact = [kept[l][name] for name in KEPT]
        acc = accs.at[l]
        w1, w2 = w1s.at[l], w2s.at[l]
        sc[D:, :] = jnp.ones((sc.shape[0] - D, W), BF)
        if first:
            acc[rows.misc :, :] = jnp.zeros((rows.total - rows.misc, D), F32)
        gpb[...] = jnp.zeros(gpb.shape, F32)
        copies.wait((l, "brs"))

        def gain(r):
            d = dy[r, :]
            put(r, 5, d * brs[r, :].astype(F32))
            gbv = (d * ff(r)).astype(BF)
            gb[r, :] = gbv
            put(r, 6, gbv.astype(F32))

        over_rows(D, gain)
        copies.wait((l, "w2"))
        up = gb[...]
        for i in range(F // FFC):
            if i * FFC % half_f == 0:
                copies.wait((l, "dact", i * FFC // half_f))
            fr = pl.ds(i * FFC, FFC)
            dact[fr, :] = (nn(w2[fr, :], up) * dact[fr, :].astype(F32)).astype(BF)
        copies.wait((l, "w1"))
        gs[...] = nn(w1[...], dact[...]).astype(BF)
        copies.wait((l, "sc"))
        if not first:
            copies.wait((l, "acc"))

        def weight_in(n, carry):
            r = nt(sc[...], dact[pl.ds(pl.multiple_of(n * 2 * D, 2 * D), 2 * D), :])
            for i in range(2):
                at = pl.ds(pl.multiple_of((2 * n + i) * D, D), D)
                part = r[:D, i * D : (i + 1) * D]
                acc[at, :] = part if first else acc[at, :] + part
            gb1[:, pl.ds(pl.multiple_of(n * 2 * D, 2 * D), 2 * D)] = r[D : D + 8]
            return carry

        lax.fori_loop(0, F // (2 * D), weight_in, 0)
        copies.wait((l, "act"))

        def weight_out(n, carry):
            r = nt(act[pl.ds(pl.multiple_of(n * 512, 512), 512), :], gb[...])
            at = pl.ds(pl.multiple_of(rows.out + n * 512, 512), 512)
            acc[at, :] = r if first else acc[at, :] + r
            return carry

        lax.fori_loop(0, F // 512, weight_out, 0)
        copies.wait((l, "mixs"), (l, "state"))

        def back(r):
            gsf = gs[r, :].astype(F32)
            mixture = mixs[r, :]
            middle = state[r, :].astype(F32) + g(r) * mixture
            gm = dy[r, :] + f(r) * gsf
            dy[r, :] = gm
            put(r, 3, gsf * middle)
            put(r, 4, gsf)
            put(r, 2, gm * mixture)
            gmb = (g(r) * gm).astype(BF)
            gb[r, :] = gmb
            gpb[...] = gpb[...] + gmb.astype(F32).reshape(ROWS // 8, 8, W).sum(0)

        over_rows(D, back)
        pbias = jnp.sum(gpb[...], 0, keepdims=True)
        copies.wait((l, "nrm"))
        for group, _, o in piece.members:
            p = patches[group]
            gi = gb[:, o : o + p]
            r0, l0 = rows.mix[group]
            acc[r0 : r0 + p, l0 : l0 + p] = acc[r0 : r0 + p, l0 : l0 + p] + tn(gi, nrm[:, o : o + p])
            gn[:, o : o + p] = nn(gi, mix[group][l])
            r0 = rows.patch[group]
            acc[r0 : r0 + 1, :p] = acc[r0 : r0 + 1, :p] + pbias[:, o : o + p]

        def pass_down(r):
            n = gn[r, :]
            put(r, 0, n * state[r, :].astype(F32))
            put(r, 1, n)
            dy[r, :] = dy[r, :] + a(r) * n

        over_rows(D, pass_down)
        acc[rows.vec : rows.vec + 8, :] = acc[rows.vec : rows.vec + 8, :] + jnp.transpose(gcol[...])[:8]
        for t in range(F // D):
            r0 = rows.bias_in + t
            acc[r0 : r0 + 1, :] = acc[r0 : r0 + 1, :] + gb1[0:1, t * D : (t + 1) * D]
        if final:
            half = rows.total // 2
            stages[l] = acc[pl.ds(pl.multiple_of((1 - core) * half, 16), half), :].astype(BF)
            copies.start((l, "send"), stages.at[l], sums_h[l][0])
            copies.start((l, "keep"), acc.at[pl.ds(pl.multiple_of(core * half, 16), half)], sums_h[l][1])
        else:
            copies.start((l, "sums"), acc, sums_h[l][0])

    for s in range(k):
        at = pl.ds(pl.multiple_of(lax.rem(me + s, k) * c, 16), c)
        outs[s][...] = dy[at, : piece.width].astype(BF)
    copies.wait_all()


def backward(piece, k, patches, rows, me, incoming, kept, w1, w2, mixes, vectors, accs, final):
    L, D, F = w1.shape
    W = piece.work
    first = accs is None
    vmem = pl.BlockSpec(memory_space=pltpu.VMEM)
    smem = pl.BlockSpec(memory_space=pltpu.SMEM)
    hbm = pl.BlockSpec(memory_space=pl.ANY)
    args = [me, *incoming, *kept, w1, w2, *[mixes[g] for g in piece.groups], *vectors]
    specs = [smem] + [vmem] * k + [hbm] * (len(kept) + 2) + [vmem] * (len(piece.groups) + len(vectors))
    if not first:
        args += accs
        specs += [hbm] * L
    out_shape = [jax.ShapeDtypeStruct((D // k, piece.width), BF)] * k
    half = rows.total // 2
    if final:
        out_shape += [jax.ShapeDtypeStruct((half, D), BF), jax.ShapeDtypeStruct((half, D), F32)] * L
    else:
        out_shape += [jax.ShapeDtypeStruct((rows.total, D), F32)] * L
    scratch = [pltpu.VMEM(*v) for l in range(L) for v in with_ones(kept_shapes(l, D, F, W), D, W).values()]
    scratch += [
        pltpu.VMEM((D, W), F32),
        pltpu.VMEM((D, W), BF),
        pltpu.VMEM((D, W), BF),
        pltpu.VMEM((D, W), F32),
        pltpu.VMEM((L, D, F), BF),
        pltpu.VMEM((L, F, D), BF),
        pltpu.VMEM((L, rows.total, D), F32),
        pltpu.VMEM((L, half, D) if final else (8, 128), BF),
        pltpu.VMEM((8, F), F32),
        pltpu.VMEM((D, 128), F32),
        pltpu.VMEM((8, W), F32),
        pltpu.VMEM((128, D), F32),
        pltpu.VMEM((L, D, 128), F32),
        pltpu.SemaphoreType.DMA((13 * L,)),
    ]
    out = pl.pallas_call(
        functools.partial(backward_kernel, piece, k, patches, rows, L, first, final),
        out_shape=out_shape,
        in_specs=specs,
        out_specs=[vmem] * k + [hbm] * (len(out_shape) - k),
        scratch_shapes=scratch,
        compiler_params=pltpu.CompilerParams(vmem_limit_bytes=VMEM_LIMIT),
        name="backward",
    )(*args)
    sums = out[k:]
    n = 2 if final else 1
    return out[:k], [sums[l * n : (l + 1) * n] for l in range(L)]


def after(value, *events):
    return lax.optimization_barrier((value, events))[0]


def flip(v, bit, n):
    return lax.ppermute(v, "dp", [(i, i ^ bit) for i in range(n)])


def cycle(v, s, k):
    return lax.ppermute(v, "swap", [(i, (i + s) % k) for i in range(k)])


def spread(bufs, distances=None):
    return [cycle(bufs[s], s, len(bufs)) if s else bufs[0] for s in distances or range(len(bufs))]


def local(body, pos, ins, shapes, name):
    vmem = pl.BlockSpec(memory_space=pltpu.VMEM)
    return pl.pallas_call(
        body,
        out_shape=[jax.ShapeDtypeStruct(*shape) for shape in shapes],
        in_specs=[pl.BlockSpec(memory_space=pltpu.SMEM)] + [vmem] * len(ins),
        out_specs=[vmem] * len(shapes),
        compiler_params=pltpu.CompilerParams(vmem_limit_bytes=40 << 20),
        name=name,
    )(pos, *ins)


def side(pos_ref, bit):
    return lax.rem(lax.div(pos_ref[1], bit), 2)


def split_first(pos, keep, came, bits):
    n, r, d = keep.shape
    q = n // 4

    def body(pos_ref, keep_ref, came_ref, *outs):
        for h in range(2):
            mine = side(pos_ref, bits[h])
            at = pl.ds(2 * q * h + mine * q, q)
            outs[2 * h][...] = keep_ref[at] + came_ref[at].astype(F32)
            at = pl.ds(2 * q * h + (1 - mine) * q, q)
            outs[2 * h + 1][...] = (keep_ref[at] + came_ref[at].astype(F32)).astype(BF)

    out = local(body, pos, [keep, came], [((q, r, d), F32), ((q, r, d), BF)] * 2, "split")
    return [(out[0], out[1]), (out[2], out[3])]


def split_next(pos, keeps, cames, bits):
    n, r, d = keeps[0].shape
    q = n // 2

    def body(pos_ref, k0, k1, c0, c1, *outs):
        for h, (keep_ref, came_ref) in enumerate(((k0, c0), (k1, c1))):
            mine = side(pos_ref, bits[h])
            at = pl.ds(mine * q, q)
            outs[2 * h][...] = keep_ref[at] + came_ref[at].astype(F32)
            at = pl.ds((1 - mine) * q, q)
            outs[2 * h + 1][...] = (keep_ref[at] + came_ref[at].astype(F32)).astype(BF)

    out = local(body, pos, [*keeps, *cames], [((q, r, d), F32), ((q, r, d), BF)] * 2, "split")
    return [(out[0], out[1]), (out[2], out[3])]


def split_swap(pos, keeps, cames, k):
    n, r, d = keeps[0].shape

    def body(pos_ref, k0, k1, c0, c1, *refs):
        outs, both = refs[:k], refs[k]
        both[:n] = k0[...] + c0[...].astype(F32)
        both[n:] = k1[...] + c1[...].astype(F32)
        me = pos_ref[0]
        outs[0][...] = both[me]
        for s in range(1, k):
            outs[s][...] = both[lax.rem(me + s, k)].astype(BF)

    vmem = pl.BlockSpec(memory_space=pltpu.VMEM)
    return pl.pallas_call(
        body,
        out_shape=[jax.ShapeDtypeStruct((r, d), F32)] + [jax.ShapeDtypeStruct((r, d), BF)] * (k - 1),
        in_specs=[pl.BlockSpec(memory_space=pltpu.SMEM)] + [vmem] * 4,
        out_specs=[vmem] * k,
        scratch_shapes=[pltpu.VMEM((2 * n, r, d), F32)],
        name="split_swap",
    )(pos, *keeps, *cames)


def add_swap(pos, keep, cames):
    def body(pos_ref, keep_ref, *refs):
        total = keep_ref[...]
        for came in refs[:-1]:
            total = total + came[...].astype(F32)
        refs[-1][...] = total.astype(BF)

    return local(body, pos, [keep, *cames], [(keep.shape, BF)], "add_swap")[0]


def join_swap(pos, parts, k):
    r, d = parts[0].shape
    n = k // 2

    def body(pos_ref, *refs):
        ins, (o0, o1), both = refs[:k], refs[k : k + 2], refs[k + 2]
        for s in range(k):
            both[lax.rem(pos_ref[0] - s + k, k)] = ins[s][...]
        o0[...] = both[:n]
        o1[...] = both[n:]

    vmem = pl.BlockSpec(memory_space=pltpu.VMEM)
    return pl.pallas_call(
        body,
        out_shape=[jax.ShapeDtypeStruct((n, r, d), BF)] * 2,
        in_specs=[pl.BlockSpec(memory_space=pltpu.SMEM)] + [vmem] * k,
        out_specs=[vmem] * 2,
        scratch_shapes=[pltpu.VMEM((k, r, d), BF)],
        name="join_swap",
    )(pos, *parts)


def join(pos, owns, cames, bits, whole):
    q, r, d = owns[0].shape

    def body(pos_ref, v0, v1, c0, c1, *outs):
        for h, (own, came) in enumerate(((v0, c0), (v1, c1))):
            mine = side(pos_ref, bits[h])
            out, base = (outs[0], 2 * q * h) if whole else (outs[h], 0)
            out[pl.ds(base + mine * q, q)] = own[...]
            out[pl.ds(base + (1 - mine) * q, q)] = came[...]

    shapes = [((4 * q, r, d), BF)] if whole else [((2 * q, r, d), BF)] * 2
    return local(body, pos, [*owns, *cames], shapes, "join")


def finish(pos, rows, ff, layer, layers, patches, mine, other, before):
    r, d = rows.total, mine.shape[-1]
    half = r // 2
    nm = rows.used - rows.misc
    last = layer == 0
    big = [(layers, d, ff), (layers, ff, d)]
    small = [(layers, d)] * 7 + [(layers, ff)] + [(layers, p) for p in patches] + [(p, layers, p) for p in patches]
    kept = before[:2]
    miscs = before[2:]

    def body(pos_ref, a_ref, b_ref, *refs):
        refs = refs[len(kept) :]
        misc_refs, refs = refs[: len(miscs)], refs[len(miscs) :]
        outs, rest, (full, win, sem) = refs[:2], refs[2:-3], refs[-3:]
        core = lax.rem(pos_ref[1], 2)
        full[pl.ds(pl.multiple_of(core * half, 16), half), :] = a_ref[...].astype(F32)
        full[pl.ds(pl.multiple_of((1 - core) * half, 16), half), :] = b_ref[...].astype(F32)
        copies = [pltpu.make_async_copy(full.at[pl.ds(rows.out, ff)], outs[1].at[layer], sem.at[1])]
        copies[0].start()
        for t in range(ff // d):
            win[:, t * d : (t + 1) * d] = full[t * d : (t + 1) * d, :]
        copies.append(pltpu.make_async_copy(win, outs[0].at[layer], sem.at[0]))
        copies[1].start()
        if last:
            sources = [(layers - 1 - i, ref, 0) for i, ref in enumerate(misc_refs)] + [(0, full, rows.misc)]
            for l, ref, base in sources:
                for j in range(7):
                    at = rows.vec - rows.misc + base + j
                    rest[j][l : l + 1, :] = ref[at : at + 1, :]
                for t in range(ff // d):
                    at = rows.bias_in - rows.misc + base + t
                    rest[7][l : l + 1, t * d : (t + 1) * d] = ref[at : at + 1, :]
                for g, p in enumerate(patches):
                    at = rows.patch[g] - rows.misc + base
                    rest[8 + g][l : l + 1, :] = ref[at : at + 1, :p]
                    at, l0 = rows.mix[g][0] - rows.misc + base, rows.mix[g][1]
                    rest[11 + g][:, l, :] = ref[at : at + p, l0 : l0 + p]
        else:
            rest[0][...] = full[rows.misc : rows.used, :]
        for cp in copies:
            cp.wait()

    vmem = pl.BlockSpec(memory_space=pltpu.VMEM)
    hbm = pl.BlockSpec(memory_space=pl.ANY)
    shapes = big + (small if last else [(nm, d)])
    out = pl.pallas_call(
        body,
        out_shape=[jax.ShapeDtypeStruct(shape, F32) for shape in shapes],
        in_specs=[pl.BlockSpec(memory_space=pltpu.SMEM), vmem, vmem] + [hbm] * len(kept) + [vmem] * len(miscs),
        out_specs=[hbm] * 2 + [vmem] * (len(shapes) - 2),
        scratch_shapes=[pltpu.VMEM((r, d), F32), pltpu.VMEM((d, ff), F32), pltpu.SemaphoreType.DMA((2,))],
        input_output_aliases={3 + i: i for i in range(len(kept))},
        compiler_params=pltpu.CompilerParams(vmem_limit_bytes=40 << 20),
        name="finish",
    )(pos, mine, other, *kept, *miscs)
    return out if last else [*out[:2], *miscs, out[2]]


def orders(n):
    bits = [1 << i for i in range(1, n.bit_length() - 1)]
    return list(zip(bits, bits[::-1]))


class Chain:
    def __init__(self, pos, rows, n, k):
        self.pos, self.rows, self.n, self.k = pos, rows, n, k
        self.steps = orders(n)

    def begin(self, send, keep):
        view = (self.rows.blocks // 2, self.rows.block, send.shape[-1])
        self.keep, self.came = keep.reshape(view), flip(send, 1, self.n).reshape(view)

    def ready(self, *events):
        self.came = after(self.came, events)

    def split(self, t):
        if t == 0:
            halves = split_first(self.pos, self.keep, self.came, self.steps[0])
        else:
            halves = split_next(self.pos, self.keep, self.came, self.steps[t])
        self.keep = [h[0] for h in halves]
        self.came = [flip(h[1], bit, self.n) for h, bit in zip(halves, self.steps[t])]
        return halves

    def split_swap(self):
        parts = split_swap(self.pos, self.keep, self.came, self.k)
        self.keep, self.came = parts[0], [cycle(parts[s], s, self.k) for s in range(1, self.k)]
        return parts

    def add_swap(self):
        self.keep = add_swap(self.pos, self.keep, self.came)
        self.came = [cycle(self.keep, s, self.k) for s in range(1, self.k)]
        return self.keep

    def join_swap(self):
        self.keep = join_swap(self.pos, [self.keep, *self.came], self.k)
        self.came = [flip(v, bit, self.n) for v, bit in zip(self.keep, self.steps[-1])]
        return self.keep

    def join(self, t):
        self.keep = join(self.pos, self.keep, self.came, self.steps[t], t == 0)
        if t > 0:
            self.came = [flip(v, bit, self.n) for v, bit in zip(self.keep, self.steps[t - 1])]
        else:
            self.keep = self.keep[0].reshape(-1, self.keep[0].shape[-1])
            self.came = flip(self.keep, 1, self.n)
        return self.keep


def on_device(
    n_dp,
    k,
    source_tiles_smallest,
    source_tiles_moderate,
    source_tiles_largest,
    target_cotangent_smallest,
    target_cotangent_moderate,
    target_cotangent_largest,
    surviving_tallies,
    token_affine_factor,
    token_affine_addend,
    crosstile_matrix_smallest,
    crosstile_matrix_moderate,
    crosstile_matrix_largest,
    crosstile_addend_smallest,
    crosstile_addend_moderate,
    crosstile_addend_largest,
    token_blend_factor,
    feedforward_affine_factor,
    feedforward_affine_addend,
    widening_matrix,
    widening_addend,
    narrowing_matrix,
    narrowing_addend,
    feedforward_factor,
):
    L, D, F = widening_matrix.shape
    tensors = [source_tiles_smallest, source_tiles_moderate, source_tiles_largest]
    cotans = [target_cotangent_smallest, target_cotangent_moderate, target_cotangent_largest]
    mixes = [crosstile_matrix_smallest, crosstile_matrix_moderate, crosstile_matrix_largest]
    biases = [crosstile_addend_smallest, crosstile_addend_moderate, crosstile_addend_largest]
    patches = [t.shape[0] for t in tensors]
    images = [t.shape[1] for t in tensors]
    own = [count // k for count in images]
    idx = lax.axis_index("dp")
    pos = lax.axis_index("swap")
    me = jnp.stack([pos, idx]).astype(jnp.int32)
    live = surviving_tallies[0]

    pieces = [
        Piece([(2, i) for i in range(own[2])] + [(0, i) for i in range(1, own[0])], patches),
        Piece([(1, i) for i in range(own[1])] + [(0, 0)], patches),
    ]
    rows = Rows(F, D, patches, n_dp * k)

    tensors = [jnp.transpose(t, (1, 2, 0)) for t in tensors]
    cotans = [jnp.transpose(t, (1, 2, 0)) for t in cotans]
    vectors = [
        token_affine_factor,
        token_affine_addend,
        token_blend_factor,
        feedforward_affine_factor,
        feedforward_affine_addend,
        feedforward_factor,
        narrowing_addend,
    ]
    w1, w2 = widening_matrix, narrowing_matrix

    first, second = pieces
    mixes = [with_layout_constraint(m, Layout((0, 1, 2))) for m in mixes]
    x_bufs = [pack(piece, k, patches, me, live, tensors, False) for piece in pieces]
    c_bufs = [pack(piece, k, patches, me, live, cotans, True) for piece in pieces]
    far = [k // 2]
    near = [s for s in range(1, k) if s != k // 2]

    x_first = after(spread(x_bufs[0]), (mixes, x_bufs[1], c_bufs))
    x_second = spread(after(x_bufs[1], x_first))
    out_first, kept_first = forward(first, k, patches, me, x_first, w1, w2, mixes, biases, vectors, widening_addend)
    x_second = after(x_second, out_first)
    c_first = spread(after(c_bufs[0], x_second))
    out_second, kept_second = forward(second, k, patches, me, x_second, w1, w2, mixes, biases, vectors, widening_addend)
    c_first = after(c_first, out_second)
    c_second = spread(after(c_bufs[1], c_first))
    came = {0: out_first[0]}
    came.update(zip(near, spread(after(out_first, c_first), near)))
    grad_first, sums = backward(first, k, patches, rows, me, c_first, kept_first, w1, w2, mixes, vectors, None, False)
    accs = [v[0] for v in sums]
    c_second, came = after((c_second, came), grad_first)
    came.update(zip(far, spread(after(out_first, c_second), far)))
    out_first = [came[s] for s in range(k)]
    out_second = spread(after(out_second, c_second))
    grad_second, halves = backward(second, k, patches, rows, me, c_second, kept_second, w1, w2, mixes, vectors, accs, True)
    out_first, out_second = after((out_first, out_second), grad_second)

    halves, grad_first = after((halves, grad_first), (out_first, out_second))
    came = {0: grad_first[0]}
    came.update(zip(near + far, spread(grad_first, near + far)))
    grad_first = [came[s] for s in range(k)]
    order = list(reversed(range(L)))
    chains = [Chain(me, rows, n_dp, k) for _ in order]
    for chain, l in zip(chains, order):
        chain.begin(*halves[l])
    token = ()

    def turn(step, *events):
        nonlocal token
        for i, chain in enumerate(chains):
            then = events[i] if i < len(events) else ()
            chain.ready(token, then() if callable(then) else then)
            token = step(chain)

    outs = [None] * 6
    alone = [g for g in range(3) if g not in second.groups]

    def arrange(base, used, groups, bufs, masked):
        chosen = [pieces[i] for i in used]
        got = unpack(chosen, groups, k, patches, images, me, live, [bufs[i] for i in used], masked)
        for i, g in enumerate(groups):
            outs[base + g] = got[i]
        return got

    count = len(orders(n_dp))
    for t in range(count):
        turn(lambda chain: chain.split(t), [came[s] for s in near] if t == 1 else ())
    turn(lambda chain: chain.split_swap(), grad_first)
    turn(lambda chain: chain.add_swap(), (), lambda: arrange(0, (0,), alone, (after(out_first, token),), True))
    turn(
        lambda chain: chain.join_swap(),
        (),
        lambda: (
            arrange(0, (0, 1), second.groups, (after(out_first, token), out_second), True),
            arrange(3, (0,), alone, (after(grad_first, token),), False),
            chains[0].came,
        ),
    )
    came = {0: grad_second[0]}
    came.update(zip(near + far, spread(after(grad_second, token), near + far)))
    grad_second = [came[s] for s in range(k)]
    for t in reversed(range(count)):
        late = [came[s] for s in (near if t == count - 1 else far if t == 0 else [])]
        turn(lambda chain: chain.join(t), (), late)
    token = arrange(3, (0, 1), second.groups, (grad_first, after(grad_second, token)), False)
    sums = []
    for chain, l in zip(chains, order):
        chain.ready(token, sums)
        sums = finish(me, rows, F, l, L, patches, chain.keep, chain.came, sums)
    outs = [jnp.transpose(v, (2, 0, 1)) for v in outs]
    grad_in, grad_out, *small = sums
    vec, bias_in, patch_bias, mix_of = small[:7], small[7], small[8:11], small[11:]
    mix_of = [jnp.transpose(v, (1, 0, 2)) for v in mix_of]

    return (
        *outs,
        vec[0],
        vec[1],
        *mix_of,
        *patch_bias,
        vec[2],
        vec[3],
        vec[4],
        grad_in,
        bias_in,
        grad_out,
        vec[6],
        vec[5],
    )


def solution(mesh):
    tokens = P(None, "dp", "swap")
    in_specs = (tokens,) * 6 + (P("dp", None),) + (P(),) * 16
    out_specs = (tokens,) * 6 + (P(),) * 16
    return jax.shard_map(
        functools.partial(on_device, mesh.shape["dp"], mesh.shape["swap"]),
        mesh=mesh,
        in_specs=in_specs,
        out_specs=out_specs,
        check_vma=False,
    )
```

profile of v0, /device:TPU:1, one launch (start us, length us, event | category | flops | bytes accessed | tf_op | source)
XLA Modules:
  0.0 275.1 jit_solution(18101099473991414456)
XLA Ops:
  4.5 2.2 collective-permute-start
  6.7 2.3 collective-permute-start.1
  13.1 1.9 copy.49.refs_8_.refs_22_
  24.9 4.9 %collective-permute-start.3 = (bf16[96,1280]{1,0:T(8,128)(2,1)}, bf16[96,1280]{1,0:T(8,128)(2,1)}, u32[]{:S(2)}, u32[]{:S(2)}) collective-permute-start(bf16[96,1280]{1,0:T(8,128)(2,1)} %get-tuple-element.268), channel_id=1, source_target_pairs={{0,1},{1,2},{2,3},{3,0},{4,5},{5,6},{6,7},{7,4},{8,9},{9,10},{10,1... | collective-permute-start | bytes 737288 | tf_op jit(solution)/shard_map/ppermute | solution.py:532
  30.2 1.9 collective-permute-start.5
  32.1 18.9 %forward.2 = (bf16[96,1152]{1,0:T(8,128)(2,1)}, bf16[96,1152]{1,0:T(8,128)(2,1)}, bf16[96,1152]{1,0:T(8,128)(2,1)}, bf16[96,1152]{1,0:T(8,128)(2,1)}, bf16[384,1...) custom-call(s32[2]{0:T(128)} %copy-done.10, ...), custom_call_target="tpu_custom_call" | custom-call | tf_op jit(solution)/shard_map/forward/pallas_call | solution.py:307
  54.8 19.9 %forward.3 = (bf16[96,1280]{1,0:T(8,128)(2,1)}, bf16[96,1280]{1,0:T(8,128)(2,1)}, bf16[96,1280]{1,0:T(8,128)(2,1)}, bf16[96,1280]{1,0:T(8,128)(2,1)}, bf16[384,1...) custom-call(s32[2]{0:T(128)} %copy-done.10, ...), custom_call_target="tpu_custom_call" | custom-call | tf_op jit(solution)/shard_map/forward/pallas_call | solution.py:307
  78.3 3.1 %collective-permute-start.13 = (bf16[96,1152]{1,0:T(8,128)(2,1)}, bf16[96,1152]{1,0:T(8,128)(2,1)}, u32[]{:S(2)}, u32[]{:S(2)}) collective-permute-start(bf16[96,1152]{1,0:T(8,128)(2,1)} %get-tuple-element.296), channel_id=1, source_target_pairs={{0,3},{1,0},{2,1},{3,2},{4,7},{5,4},{6,5},{7,6},{8,11},{9,8},{10,9... | collective-permute-start | bytes 663560 | tf_op jit(solution)/shard_map/ppermute | solution.py:532
  81.4 33.2 %backward.2 = (bf16[96,1152]{1,0:T(8,128)(2,1)}, bf16[96,1152]{1,0:T(8,128)(2,1)}, bf16[96,1152]{1,0:T(8,128)(2,1)}, bf16[96,1152]{1,0:T(8,128)(2,1)}, f32[3840,384]{1,0:T(8,128)}, /*index=5*/f32[3840,384]{1,0:T(8,128)}) custom-call(s32[2]{0:T(128)} %copy-done.10, bf16[96,1152]{1,0:T(8,128)(2,1)} %copy-done.25, ...), custom_call_target="tpu_custom_call" | custom-call | tf_op jit(solution)/shard_map/backward/pallas_call | solution.py:509
  115.0 3.0 %collective-permute-start.17 = (bf16[96,1280]{1,0:T(8,128)(2,1)}, bf16[96,1280]{1,0:T(8,128)(2,1)}, u32[]{:S(2)}, u32[]{:S(2)}) collective-permute-start(bf16[96,1280]{1,0:T(8,128)(2,1)} %get-tuple-element.326), channel_id=1, source_target_pairs={{0,3},{1,0},{2,1},{3,2},{4,7},{5,4},{6,5},{7,6},{8,11},{9,8},{10,9... | collective-permute-start | bytes 737288 | tf_op jit(solution)/shard_map/ppermute | solution.py:532
  119.4 35.3 %backward.3 = (bf16[96,1280]{1,0:T(8,128)(2,1)}, bf16[96,1280]{1,0:T(8,128)(2,1)}, bf16[96,1280]{1,0:T(8,128)(2,1)}, bf16[96,1280]{1,0:T(8,128)(2,1)}, bf16[1920...) custom-call(s32[2]{0:T(128)} %copy-done.10, ...), custom_call_target="tpu_custom_call" | custom-call | tf_op jit(solution)/shard_map/backward/pallas_call | solution.py:509
  154.8 4.5 %collective-permute-start.18 = (bf16[1920,384]{1,0:T(8,128)(2,1)}, bf16[1920,384]{1,0:T(8,128)(2,1)S(1)}, u32[]{:S(2)}, u32[]{:S(2)}) collective-permute-start(bf16[1920,384]{1,0:T(8,128)(2,1)} %get-tuple-element.360), channel_id=1, source_target_pairs={{0,4},{4,0},{8,12},{12,8},{16,20},{20,16},{24,28},{28,24},{1,5},{5... | collective-permute-start | bytes 4423688 | tf_op jit(solution)/shard_map/ppermute | solution.py:528
  159.4 3.0 %collective-permute-done.18 = bf16[1920,384]{1,0:T(8,128)(2,1)S(1)} collective-permute-done((bf16[1920,384]{1,0:T(8,128)(2,1)}, bf16[1920,384]{1,0:T(8,128)(2,1)S(1)}, u32[]{:S(2)}, u32[]{:S(2)}) %collective-permute-start.18) | collective-permute-done | bytes 1474592 | tf_op jit(solution)/shard_map/ppermute | solution.py:528
  162.4 1.8 copy-done.1
  170.3 4.8 %collective-permute-done.23.refs_3_ = bf16[96,1152]{1,0:T(8,128)(2,1)S(1)} collective-permute-done((bf16[96,1152]{1,0:T(8,128)(2,1)S(1)}, bf16[96,1152]{1,0:T(8,128)(2,1)S(1)}, u32[]{:S(2)}, u32[]{:S(2)}) %collective-permute-start.23) | collective-permute-done | bytes 221216 | tf_op jit(solution)/shard_map/ppermute | solution.py:532
  179.7 3.9 %collective-permute-done.26.c0 = bf16[4,120,384]{2,1,0:T(8,128)(2,1)S(1)} collective-permute-done((bf16[4,120,384]{2,1,0:T(8,128)(2,1)S(1)}, bf16[4,120,384]{2,1,0:T(8,128)(2,1)S(1)}, u32[]{:S(2)}, u32[]{:S(2)}) %collective-permute-start.26) | collective-permute-done | bytes 368672 | tf_op jit(solution)/shard_map/ppermute | solution.py:528
  189.1 2.0 split_swap.2
  192.3 2.2 collective-permute-start.31
  195.2 2.1 split_swap.3
  198.8 2.3 collective-permute-start.39
  205.1 2.5 unpack.4
  208.2 8.8 %collective-permute-done.35.refs_2_ = bf16[120,384]{1,0:T(8,128)(2,1)S(1)} collective-permute-done((bf16[120,384]{1,0:T(8,128)(2,1)S(1)}, bf16[120,384]{1,0:T(8,128)(2,1)S(1)}, u32[]{:S(2)}, u32[]{:S(2)}) %collective-permute-start.35) | collective-permute-done | bytes 92192 | tf_op jit(solution)/shard_map/ppermute | solution.py:532
  226.1 4.4 %unpack.5 = (f32[24,96,100]{2,1,0:T(8,128)}, f32[24,96,196]{2,1,0:T(8,128)}) custom-call(s32[2]{0:T(128)S(1)} %copy-done.13, s32[3]{0:T(128)S(1)} %bitcast.46, bf16[96,1152]{1,0:T(8,128)(2,1)S(1)} %copy-done.7, bf16[96,1152]{1,0:T(8,128)(2,1)} %collective-permute-done.12.refs_1_, bf16[96,1152]{1,0:T(8,128)(2,1)} %collective-permute-done.14.refs_2_, ...), custom_call_target="tpu_custom_call" | custom-call | tf_op jit(solution)/shard_map/unpack/pallas_call | solution.py:102
  234.0 2.5 collective-permute-start.47
  238.8 2.7 collective-permute-done.48.c0
  241.5 4.4 %collective-permute-done.47.refs_7_ = bf16[96,1280]{1,0:T(8,128)(2,1)S(1)} collective-permute-done((bf16[96,1280]{1,0:T(8,128)(2,1)S(1)}, bf16[96,1280]{1,0:T(8,128)(2,1)S(1)}, u32[]{:S(2)}, u32[]{:S(2)}) %collective-permute-start.47) | collective-permute-done | bytes 245792 | tf_op jit(solution)/shard_map/ppermute | solution.py:532
  250.3 8.9 %collective-permute-start.55 = (bf16[1920,384]{1,0:T(8,128)(2,1)S(1)}, bf16[1920,384]{1,0:T(8,128)(2,1)S(1)}, u32[]{:S(2)}, u32[]{:S(2)}) collective-permute-start(bf16[1920,384]{1,0:T(8,128)(2,1)S(1)} %bitcast.26), channel_id=1, source_target_pairs={{0,4},{4,0},{8,12},{12,8},{16,20},{20,16},{24,28},{28,24},{1,5},{5... | collective-permute-start | bytes 4423688 | tf_op jit(solution)/shard_map/ppermute | solution.py:528
  259.2 2.2 collective-permute-done.46.refs_6_
  262.1 1.9 collective-permute-start.54
  264.0 3.0 %unpack.7 = (f32[24,96,100]{2,1,0:T(8,128)}, f32[24,96,196]{2,1,0:T(8,128)}) custom-call(s32[2]{0:T(128)S(1)} %copy-done.14, s32[3]{0:T(128)S(1)} %bitcast.47, bf16[96,1152]{1,0:T(8,128)(2,1)S(1)} %copy-done.6, bf16[96,1152]{1,0:T(8,128)(2,1)S(1)} %collective-permute-done.22.refs_1_, bf16[96,1152]{1,0:T(8,128)(2,1)S(1)} %collective-permute-done.28.refs_2_, ...), custom_call_target="tpu_custom_call" | custom-call | tf_op jit(solution)/shard_map/unpack/pallas_call | solution.py:102
  266.9 3.3 %finish.2 = (f32[2,384,1536]{2,1,0:T(8,128)}, f32[2,1536,384]{2,1,0:T(8,128)}, f32[544,384]{1,0:T(8,128)S(1)}) custom-call(s32[2]{0:T(128)S(1)} %copy-done.14, bf16[1920,384]{1,0:T(8,128)(2,1)S(1)} %bitcast.27, bf16[1920,384]{1,0:T(8,128)(2,1)S(1)} %collective-permute-done.55.b_ref), custom_call_target="tpu_custom_call" | custom-call | tf_op jit(solution)/shard_map/finish/pallas_call | solution.py:701
  270.3 4.5 %finish.3 = (f32[2,384,1536]{2,1,0:T(8,128)}, f32[2,1536,384]{2,1,0:T(8,128)}, f32[2,384]{1,0:T(2,128)}, f32[2,384]{1,0:T(2,128)}, f32[2,384]{1,0:T(2,128)}, /*i...) custom-call(s32[2]{0:T(128)S(1)} %copy-done.14, ...), custom_call_target="tpu_custom_call", output_to_operand_aliasing={{0}: (3, {}), {1}: (4, {})} | custom-call | tf_op jit(solution)/shard_map/finish/pallas_call | solution.py:701
  (230 shorter events, 71.2 us)
Async XLA Ops:
  4.5 19.0 %collective-permute-start = (bf16[96,1152]{1,0:T(8,128)(2,1)S(1)}, bf16[96,1152]{1,0:T(8,128)(2,1)S(1)}, u32[]{:S(2)}, u32[]{:S(2)}) collective-permute-start(bf16[96,1152]{1,0:T(8,128)(2,1)S(1)} %get-tuple-element.260), channel_id=1, source_target_pairs={{0,1},{1,2},{2,3},{3,0},{4,5},{5,6},{6,7},{7,4},{8,9},{9,10},{10,1... | collective-permute-start | bytes 663560 | tf_op jit(solution)/shard_map/ppermute | solution.py:532
  6.7 17.4 %collective-permute-start.1 = (bf16[96,1152]{1,0:T(8,128)(2,1)S(1)}, bf16[96,1152]{1,0:T(8,128)(2,1)S(1)}, u32[]{:S(2)}, u32[]{:S(2)}) collective-permute-start(bf16[96,1152]{1,0:T(8,128)(2,1)S(1)} %get-tuple-element.261), channel_id=1, source_target_pairs={{0,2},{1,3},{2,0},{3,1},{4,6},{5,7},{6,4},{7,5},{8,10},{9,11},{10,... | collective-permute-start | bytes 663560 | tf_op jit(solution)/shard_map/ppermute | solution.py:532
  9.0 15.1 %collective-permute-start.2 = (bf16[96,1152]{1,0:T(8,128)(2,1)S(1)}, bf16[96,1152]{1,0:T(8,128)(2,1)S(1)}, u32[]{:S(2)}, u32[]{:S(2)}) collective-permute-start(bf16[96,1152]{1,0:T(8,128)(2,1)S(1)} %get-tuple-element.262), channel_id=1, source_target_pairs={{0,3},{1,0},{2,1},{3,2},{4,7},{5,4},{6,5},{7,6},{8,11},{9,8},{10,9... | collective-permute-start | bytes 663560 | tf_op jit(solution)/shard_map/ppermute | solution.py:532
  24.9 26.0 %collective-permute-start.3 = (bf16[96,1280]{1,0:T(8,128)(2,1)}, bf16[96,1280]{1,0:T(8,128)(2,1)}, u32[]{:S(2)}, u32[]{:S(2)}) collective-permute-start(bf16[96,1280]{1,0:T(8,128)(2,1)} %get-tuple-element.268), channel_id=1, source_target_pairs={{0,1},{1,2},{2,3},{3,0},{4,5},{5,6},{6,7},{7,4},{8,9},{9,10},{10,1... | collective-permute-start | bytes 737288 | tf_op jit(solution)/shard_map/ppermute | solution.py:532
  29.9 21.1 %collective-permute-start.4 = (bf16[96,1280]{1,0:T(8,128)(2,1)}, bf16[96,1280]{1,0:T(8,128)(2,1)}, u32[]{:S(2)}, u32[]{:S(2)}) collective-permute-start(bf16[96,1280]{1,0:T(8,128)(2,1)} %get-tuple-element.269), channel_id=1, source_target_pairs={{0,2},{1,3},{2,0},{3,1},{4,6},{5,7},{6,4},{7,5},{8,10},{9,11},{10,... | collective-permute-start | bytes 737288 | tf_op jit(solution)/shard_map/ppermute | solution.py:532
  30.2 20.8 %collective-permute-start.5 = (bf16[96,1280]{1,0:T(8,128)(2,1)}, bf16[96,1280]{1,0:T(8,128)(2,1)}, u32[]{:S(2)}, u32[]{:S(2)}) collective-permute-start(bf16[96,1280]{1,0:T(8,128)(2,1)} %get-tuple-element.270), channel_id=1, source_target_pairs={{0,3},{1,0},{2,1},{3,2},{4,7},{5,4},{6,5},{7,6},{8,11},{9,8},{10,9... | collective-permute-start | bytes 737288 | tf_op jit(solution)/shard_map/ppermute | solution.py:532
  51.0 23.7 %collective-permute-start.6 = (bf16[96,1152]{1,0:T(8,128)(2,1)}, bf16[96,1152]{1,0:T(8,128)(2,1)}, u32[]{:S(2)}, u32[]{:S(2)}) collective-permute-start(bf16[96,1152]{1,0:T(8,128)(2,1)} %copy-done.40), channel_id=1, source_target_pairs={{0,1},{1,2},{2,3},{3,0},{4,5},{5,6},{6,7},{7,4},{8,9},{9,10},{10,1... | collective-permute-start | bytes 663560 | tf_op jit(solution)/shard_map/ppermute | solution.py:532
  52.7 22.0 %collective-permute-start.7 = (bf16[96,1152]{1,0:T(8,128)(2,1)}, bf16[96,1152]{1,0:T(8,128)(2,1)}, u32[]{:S(2)}, u32[]{:S(2)}) collective-permute-start(bf16[96,1152]{1,0:T(8,128)(2,1)} %copy-done.39), channel_id=1, source_target_pairs={{0,2},{1,3},{2,0},{3,1},{4,6},{5,7},{6,4},{7,5},{8,10},{9,11},{10,... | collective-permute-start | bytes 663560 | tf_op jit(solution)/shard_map/ppermute | solution.py:532
  54.2 20.5 %collective-permute-start.8 = (bf16[96,1152]{1,0:T(8,128)(2,1)}, bf16[96,1152]{1,0:T(8,128)(2,1)}, u32[]{:S(2)}, u32[]{:S(2)}) collective-permute-start(bf16[96,1152]{1,0:T(8,128)(2,1)} %copy-done.38), channel_id=1, source_target_pairs={{0,3},{1,0},{2,1},{3,2},{4,7},{5,4},{6,5},{7,6},{8,11},{9,8},{10,9... | collective-permute-start | bytes 663560 | tf_op jit(solution)/shard_map/ppermute | solution.py:532
  74.7 39.9 %collective-permute-start.9 = (bf16[96,1280]{1,0:T(8,128)(2,1)}, bf16[96,1280]{1,0:T(8,128)(2,1)}, u32[]{:S(2)}, u32[]{:S(2)}) collective-permute-start(bf16[96,1280]{1,0:T(8,128)(2,1)} %copy-done.37), channel_id=1, source_target_pairs={{0,1},{1,2},{2,3},{3,0},{4,5},{5,6},{6,7},{7,4},{8,9},{9,10},{10,1... | collective-permute-start | bytes 737288 | tf_op jit(solution)/shard_map/ppermute | solution.py:532
  75.7 39.0 %collective-permute-start.10 = (bf16[96,1280]{1,0:T(8,128)(2,1)}, bf16[96,1280]{1,0:T(8,128)(2,1)}, u32[]{:S(2)}, u32[]{:S(2)}) collective-permute-start(bf16[96,1280]{1,0:T(8,128)(2,1)} %copy-done.36), channel_id=1, source_target_pairs={{0,2},{1,3},{2,0},{3,1},{4,6},{5,7},{6,4},{7,5},{8,10},{9,11},{10,... | collective-permute-start | bytes 737288 | tf_op jit(solution)/shard_map/ppermute | solution.py:532
  76.5 38.1 %collective-permute-start.11 = (bf16[96,1280]{1,0:T(8,128)(2,1)}, bf16[96,1280]{1,0:T(8,128)(2,1)}, u32[]{:S(2)}, u32[]{:S(2)}) collective-permute-start(bf16[96,1280]{1,0:T(8,128)(2,1)} %copy-done.35), channel_id=1, source_target_pairs={{0,3},{1,0},{2,1},{3,2},{4,7},{5,4},{6,5},{7,6},{8,11},{9,8},{10,9... | collective-permute-start | bytes 737288 | tf_op jit(solution)/shard_map/ppermute | solution.py:532
  78.1 36.5 %collective-permute-start.12 = (bf16[96,1152]{1,0:T(8,128)(2,1)}, bf16[96,1152]{1,0:T(8,128)(2,1)}, u32[]{:S(2)}, u32[]{:S(2)}) collective-permute-start(bf16[96,1152]{1,0:T(8,128)(2,1)} %get-tuple-element.295), channel_id=1, source_target_pairs={{0,1},{1,2},{2,3},{3,0},{4,5},{5,6},{6,7},{7,4},{8,9},{9,10},{10,1... | collective-permute-start | bytes 663560 | tf_op jit(solution)/shard_map/ppermute | solution.py:532
  78.3 36.3 %collective-permute-start.13 = (bf16[96,1152]{1,0:T(8,128)(2,1)}, bf16[96,1152]{1,0:T(8,128)(2,1)}, u32[]{:S(2)}, u32[]{:S(2)}) collective-permute-start(bf16[96,1152]{1,0:T(8,128)(2,1)} %get-tuple-element.296), channel_id=1, source_target_pairs={{0,3},{1,0},{2,1},{3,2},{4,7},{5,4},{6,5},{7,6},{8,11},{9,8},{10,9... | collective-permute-start | bytes 663560 | tf_op jit(solution)/shard_map/ppermute | solution.py:532
  114.7 40.1 %collective-permute-start.15 = (bf16[96,1280]{1,0:T(8,128)(2,1)}, bf16[96,1280]{1,0:T(8,128)(2,1)}, u32[]{:S(2)}, u32[]{:S(2)}) collective-permute-start(bf16[96,1280]{1,0:T(8,128)(2,1)} %get-tuple-element.324), channel_id=1, source_target_pairs={{0,1},{1,2},{2,3},{3,0},{4,5},{5,6},{6,7},{7,4},{8,9},{9,10},{10,1... | collective-permute-start | bytes 737288 | tf_op jit(solution)/shard_map/ppermute | solution.py:532
  114.7 40.1 %collective-permute-start.16 = (bf16[96,1280]{1,0:T(8,128)(2,1)}, bf16[96,1280]{1,0:T(8,128)(2,1)}, u32[]{:S(2)}, u32[]{:S(2)}) collective-permute-start(bf16[96,1280]{1,0:T(8,128)(2,1)} %get-tuple-element.325), channel_id=1, source_target_pairs={{0,2},{1,3},{2,0},{3,1},{4,6},{5,7},{6,4},{7,5},{8,10},{9,11},{10,... | collective-permute-start | bytes 737288 | tf_op jit(solution)/shard_map/ppermute | solution.py:532
  115.0 39.8 %collective-permute-start.17 = (bf16[96,1280]{1,0:T(8,128)(2,1)}, bf16[96,1280]{1,0:T(8,128)(2,1)}, u32[]{:S(2)}, u32[]{:S(2)}) collective-permute-start(bf16[96,1280]{1,0:T(8,128)(2,1)} %get-tuple-element.326), channel_id=1, source_target_pairs={{0,3},{1,0},{2,1},{3,2},{4,7},{5,4},{6,5},{7,6},{8,11},{9,8},{10,9... | collective-permute-start | bytes 737288 | tf_op jit(solution)/shard_map/ppermute | solution.py:532
  118.0 36.8 %collective-permute-start.14 = (bf16[96,1152]{1,0:T(8,128)(2,1)}, bf16[96,1152]{1,0:T(8,128)(2,1)}, u32[]{:S(2)}, u32[]{:S(2)}) collective-permute-start(bf16[96,1152]{1,0:T(8,128)(2,1)} %get-tuple-element.321), channel_id=1, source_target_pairs={{0,2},{1,3},{2,0},{3,1},{4,6},{5,7},{6,4},{7,5},{8,10},{9,11},{10,... | collective-permute-start | bytes 663560 | tf_op jit(solution)/shard_map/ppermute | solution.py:532
  159.4 10.3 %collective-permute-start.22 = (bf16[96,1152]{1,0:T(8,128)(2,1)}, bf16[96,1152]{1,0:T(8,128)(2,1)S(1)}, u32[]{:S(2)}, u32[]{:S(2)}) collective-permute-start(bf16[96,1152]{1,0:T(8,128)(2,1)} %get-tuple-element.372), channel_id=1, source_target_pairs={{0,1},{1,2},{2,3},{3,0},{4,5},{5,6},{6,7},{7,4},{8,9},{9,10},{10,1... | collective-permute-start | bytes 663560 | tf_op jit(solution)/shard_map/ppermute | solution.py:532
  169.2 14.4 %collective-permute-start.26 = (bf16[4,120,384]{2,1,0:T(8,128)(2,1)S(1)}, bf16[4,120,384]{2,1,0:T(8,128)(2,1)S(1)}, u32[]{:S(2)}, u32[]{:S(2)}) collective-permute-start(bf16[4,120,384]{2,1,0:T(8,128)(2,1)S(1)} %get-tuple-element.369), channel_id=1, source_target_pairs={{0,8},{4,12},{8,0},{12,4},{16,24},{20,28},{24,16},{28,20},{1,9},{5... | collective-permute-start | bytes 1105928 | tf_op jit(solution)/shard_map/ppermute | solution.py:528
  169.5 15.0 %collective-permute-start.27 = (bf16[4,120,384]{2,1,0:T(8,128)(2,1)S(1)}, bf16[4,120,384]{2,1,0:T(8,128)(2,1)S(1)}, u32[]{:S(2)}, u32[]{:S(2)}) collective-permute-start(bf16[4,120,384]{2,1,0:T(8,128)(2,1)S(1)} %get-tuple-element.371), channel_id=1, source_target_pairs={{0,16},{4,20},{8,24},{12,28},{16,0},{20,4},{24,8},{28,12},{1,17},{... | collective-permute-start | bytes 1105928 | tf_op jit(solution)/shard_map/ppermute | solution.py:528
  175.1 13.1 %collective-permute-start.28 = (bf16[96,1152]{1,0:T(8,128)(2,1)S(1)}, bf16[96,1152]{1,0:T(8,128)(2,1)S(1)}, u32[]{:S(2)}, u32[]{:S(2)}) collective-permute-start(bf16[96,1152]{1,0:T(8,128)(2,1)S(1)} %copy-done.57), channel_id=1, source_target_pairs={{0,2},{1,3},{2,0},{3,1},{4,6},{5,7},{6,4},{7,5},{8,10},{9,11},{10,... | collective-permute-start | bytes 663560 | tf_op jit(solution)/shard_map/ppermute | solution.py:532
  178.0 10.4 %collective-permute-start.24 = (bf16[2,120,384]{2,1,0:T(8,128)(2,1)S(1)}, bf16[2,120,384]{2,1,0:T(8,128)(2,1)S(1)}, u32[]{:S(2)}, u32[]{:S(2)}) collective-permute-start(bf16[2,120,384]{2,1,0:T(8,128)(2,1)S(1)} %get-tuple-element.378), channel_id=1, source_target_pairs={{0,16},{4,20},{8,24},{12,28},{16,0},{20,4},{24,8},{28,12},{1,17},{... | collective-permute-start | bytes 552968 | tf_op jit(solution)/shard_map/ppermute | solution.py:528
  202.7 14.3 %collective-permute-start.35 = (bf16[120,384]{1,0:T(8,128)(2,1)S(1)}, bf16[120,384]{1,0:T(8,128)(2,1)S(1)}, u32[]{:S(2)}, u32[]{:S(2)}) collective-permute-start(bf16[120,384]{1,0:T(8,128)(2,1)S(1)} %add_swap.2.refs_0_), channel_id=1, source_target_pairs={{0,2},{1,3},{2,0},{3,1},{4,6},{5,7},{6,4},{7,5},{8,10},{9,11},{10,... | collective-permute-start | bytes 276488 | tf_op jit(solution)/shard_map/ppermute | solution.py:532
  204.5 12.6 %collective-permute-start.34 = (bf16[120,384]{1,0:T(8,128)(2,1)S(1)}, bf16[120,384]{1,0:T(8,128)(2,1)S(1)}, u32[]{:S(2)}, u32[]{:S(2)}) collective-permute-start(bf16[120,384]{1,0:T(8,128)(2,1)S(1)} %add_swap.2.refs_0_), channel_id=1, source_target_pairs={{0,1},{1,2},{2,3},{3,0},{4,5},{5,6},{6,7},{7,4},{8,9},{9,10},{10,1... | collective-permute-start | bytes 276488 | tf_op jit(solution)/shard_map/ppermute | solution.py:532
  220.2 10.5 %collective-permute-start.43 = (bf16[2,120,384]{2,1,0:T(8,128)(2,1)}, bf16[2,120,384]{2,1,0:T(8,128)(2,1)S(1)}, u32[]{:S(2)}, u32[]{:S(2)}) collective-permute-start(bf16[2,120,384]{2,1,0:T(8,128)(2,1)} %get-tuple-element.413.v0), channel_id=1, source_target_pairs={{0,16},{4,20},{8,24},{12,28},{16,0},{20,4},{24,8},{28,12},{1,17},{... | collective-permute-start | bytes 552968 | tf_op jit(solution)/shard_map/ppermute | solution.py:528
  234.0 11.9 %collective-permute-start.47 = (bf16[96,1280]{1,0:T(8,128)(2,1)S(1)}, bf16[96,1280]{1,0:T(8,128)(2,1)S(1)}, u32[]{:S(2)}, u32[]{:S(2)}) collective-permute-start(bf16[96,1280]{1,0:T(8,128)(2,1)S(1)} %copy-done.55), channel_id=1, source_target_pairs={{0,3},{1,0},{2,1},{3,2},{4,7},{5,4},{6,5},{7,6},{8,11},{9,8},{10,9... | collective-permute-start | bytes 737288 | tf_op jit(solution)/shard_map/ppermute | solution.py:532
  237.7 11.3 %collective-permute-start.52 = (bf16[4,120,384]{2,1,0:T(8,128)(2,1)S(1)}, bf16[4,120,384]{2,1,0:T(8,128)(2,1)S(1)}, u32[]{:S(2)}, u32[]{:S(2)}) collective-permute-start(bf16[4,120,384]{2,1,0:T(8,128)(2,1)S(1)} %get-tuple-element.435.v0), channel_id=1, source_target_pairs={{0,8},{4,12},{8,0},{12,4},{16,24},{20,28},{24,16},{28,20},{1,9},{5... | collective-permute-start | bytes 1105928 | tf_op jit(solution)/shard_map/ppermute | solution.py:528
  248.4 13.0 %collective-permute-start.50 = (bf16[4,120,384]{2,1,0:T(8,128)(2,1)S(1)}, bf16[4,120,384]{2,1,0:T(8,128)(2,1)S(1)}, u32[]{:S(2)}, u32[]{:S(2)}) collective-permute-start(bf16[4,120,384]{2,1,0:T(8,128)(2,1)S(1)} %get-tuple-element.439.v0), channel_id=1, source_target_pairs={{0,8},{4,12},{8,0},{12,4},{16,24},{20,28},{24,16},{28,20},{1,9},{5... | collective-permute-start | bytes 1105928 | tf_op jit(solution)/shard_map/ppermute | solution.py:528
  248.5 12.9 %collective-permute-start.51 = (bf16[4,120,384]{2,1,0:T(8,128)(2,1)S(1)}, bf16[4,120,384]{2,1,0:T(8,128)(2,1)S(1)}, u32[]{:S(2)}, u32[]{:S(2)}) collective-permute-start(bf16[4,120,384]{2,1,0:T(8,128)(2,1)S(1)} %get-tuple-element.440.v1), channel_id=1, source_target_pairs={{0,16},{4,20},{8,24},{12,28},{16,0},{20,4},{24,8},{28,12},{1,17},{... | collective-permute-start | bytes 1105928 | tf_op jit(solution)/shard_map/ppermute | solution.py:528
  248.6 12.8 %collective-permute-start.46 = (bf16[96,1280]{1,0:T(8,128)(2,1)S(1)}, bf16[96,1280]{1,0:T(8,128)(2,1)S(1)}, u32[]{:S(2)}, u32[]{:S(2)}) collective-permute-start(bf16[96,1280]{1,0:T(8,128)(2,1)S(1)} %copy-done.54), channel_id=1, source_target_pairs={{0,2},{1,3},{2,0},{3,1},{4,6},{5,7},{6,4},{7,5},{8,10},{9,11},{10,... | collective-permute-start | bytes 737288 | tf_op jit(solution)/shard_map/ppermute | solution.py:532
  250.3 16.7 %collective-permute-start.55 = (bf16[1920,384]{1,0:T(8,128)(2,1)S(1)}, bf16[1920,384]{1,0:T(8,128)(2,1)S(1)}, u32[]{:S(2)}, u32[]{:S(2)}) collective-permute-start(bf16[1920,384]{1,0:T(8,128)(2,1)S(1)} %bitcast.26), channel_id=1, source_target_pairs={{0,4},{4,0},{8,12},{12,8},{16,20},{20,16},{24,28},{28,24},{1,5},{5... | collective-permute-start | bytes 4423688 | tf_op jit(solution)/shard_map/ppermute | solution.py:528
  (83 other events, 703.9 us)
where the time goes:
time: 278 us; the launch traced here: 275 us
  Pallas kernels  146 us (53%)
  starting transfers between devices  70.4 us (25%)
  waiting for transfers between devices  32.9 us (12%)
  local copies, waits for them, and re-layouts  24.3 us (9%)
    pallas_call x2, Pallas kernels, backward(): pl.pallas_call(functools.partial(backward_kernel, piece, k, patches, rows...  68.5 us
    ppermute x36, starting transfers between devices, cycle(): return lax.ppermute(v, 'swap', [(i, (i + s) % k) for i in range(k)])  44.3 us
    pallas_call x2, Pallas kernels, forward(): pl.pallas_call(functools.partial(forward_kernel, piece, k, patches, L), o...  38.7 us
    ppermute x20, starting transfers between devices, flip(): return lax.ppermute(v, 'dp', [(i, i ^ bit) for i in range(n)])  26.1 us
    unnamed x121, local copies, waits for them, and re-layouts  24.3 us
    ppermute x36, waiting for transfers between devices, cycle(): return lax.ppermute(v, 'swap', [(i, (i + s) % k) for i in range(k)])  20.9 us
    ppermute x20, waiting for transfers between devices, flip(): return lax.ppermute(v, 'dp', [(i, i ^ bit) for i in range(n)])  12 us
    pallas_call x4, Pallas kernels, unpack(): pl.pallas_call(functools.partial(unpack_kernel, pieces, groups, k, patche...  11.6 us
  transfers between devices with their start and end apart: 56, of which 12 were waited for; matrix products, arithmetic and copies ran while one was open for 2% of the time, Pallas kernels for 50%

commit v1 on v0

--- a/solution.py
+++ b/solution.py
@@ -111,22 +111,35 @@
 
 class Rows:
     def __init__(self, ff, width, patches, blocks):
+        small, medium, large = patches
         self.out = ff
-        base = 2 * ff
-        self.mix = [
-            (base + round_up(patches[2], 8), round_up(patches[1], 128)),
-            (base + round_up(patches[2], 8), 0),
-            (base, 0),
-        ]
-        self.misc = base
-        base += round_up(patches[2], 8) + round_up(patches[1], 8)
-        self.bias_in = base
-        self.patch = [base + ff // width + g for g in range(3)]
-        self.vec = round_up(base + ff // width + 3, 8)
-        self.used = self.vec + 8
+        self.misc = 2 * ff
+        self.lanes = width // 128
+        side = round_up(medium, 128)
+        top = self.misc + round_up(large, 8)
+        self.side = side
+        self.vec = top + round_up(small, 8)
+        rest = self.vec + 16 * self.lanes
+        pieces = -(-medium // (width - side))
+        span = -(-medium // pieces)
+        for cut in range(8, round_up(medium, 8) + 1, 8):
+            left = max(medium - cut, 0)
+            if rest - top + pieces * round_up(left, 8) <= cut:
+                break
+        self.mix = [[(0, small, 0, small, top, side)], [(0, min(cut, medium), 0, medium, top, 0)], [(0, large, 0, large, self.misc, 0)]]
+        for i in range(pieces if left else 0):
+            lanes = min(span, medium - i * span)
+            self.mix[1].append((cut, left, i * span, lanes, rest + i * round_up(left, 8), side))
+        self.used = top + cut
         self.blocks = blocks
         self.block = round_up(-(-self.used // blocks), 8)
         self.total = blocks * self.block
+
+    def vector(self, index, length):
+        return [(128 * q, min(128, length - 128 * q), self.vec + 16 * q + index) for q in range(-(-length // 128))]
+
+
+BIAS_IN, PATCH = 8, 12
 
 
 def over_rows(count, body):
@@ -343,7 +356,6 @@
     copies = Copies(sem)
     half_f = F // 2
     for l in reversed(range(layers)):
-        copies.start((l, "brs"), kept_h[l]["brs"], kept[l]["brs"])
         copies.start((l, "w2"), w2_h.at[l], w2s.at[l])
         for i in range(2):
             at = pl.ds(i * half_f, half_f)
@@ -352,7 +364,7 @@
         copies.start((l, "sc"), kept_h[l]["sc"], kept[l]["sc"].at[pl.ds(0, D)])
         if not first:
             copies.start((l, "acc"), accs_h[l], accs.at[l])
-        for name in ("act", "mixs", "state", "nrm"):
+        for name in ("act", "brs", "mixs", "state", "nrm"):
             copies.start((l, name), kept_h[l][name], kept[l][name])
 
     load_columns(vectors, line, cols, layers)
@@ -377,12 +389,9 @@
         if first:
             acc[rows.misc :, :] = jnp.zeros((rows.total - rows.misc, D), F32)
         gpb[...] = jnp.zeros(gpb.shape, F32)
-        copies.wait((l, "brs"))
 
         def gain(r):
-            d = dy[r, :]
-            put(r, 5, d * brs[r, :].astype(F32))
-            gbv = (d * ff(r)).astype(BF)
+            gbv = (dy[r, :] * ff(r)).astype(BF)
             gb[r, :] = gbv
             put(r, 6, gbv.astype(F32))
 
@@ -419,13 +428,15 @@
             return carry
 
         lax.fori_loop(0, F // 512, weight_out, 0)
-        copies.wait((l, "mixs"), (l, "state"))
+        copies.wait((l, "brs"), (l, "mixs"), (l, "state"))
 
         def back(r):
             gsf = gs[r, :].astype(F32)
             mixture = mixs[r, :]
             middle = state[r, :].astype(F32) + g(r) * mixture
-            gm = dy[r, :] + f(r) * gsf
+            d = dy[r, :]
+            put(r, 5, d * brs[r, :].astype(F32))
+            gm = d + f(r) * gsf
             dy[r, :] = gm
             put(r, 3, gsf * middle)
             put(r, 4, gsf)
@@ -437,14 +448,18 @@
         over_rows(D, back)
         pbias = jnp.sum(gpb[...], 0, keepdims=True)
         copies.wait((l, "nrm"))
+        side = rows.side
         for group, _, o in piece.members:
             p = patches[group]
             gi = gb[:, o : o + p]
-            r0, l0 = rows.mix[group]
-            acc[r0 : r0 + p, l0 : l0 + p] = acc[r0 : r0 + p, l0 : l0 + p] + tn(gi, nrm[:, o : o + p])
+            product = tn(gi, nrm[:, o : o + p])
+            for r0, nr, c0, nc, at, lane in rows.mix[group]:
+                part = product[r0 : r0 + nr, c0 : c0 + nc]
+                acc[at : at + nr, lane : lane + nc] = acc[at : at + nr, lane : lane + nc] + part
             gn[:, o : o + p] = nn(gi, mix[group][l])
-            r0 = rows.patch[group]
-            acc[r0 : r0 + 1, :p] = acc[r0 : r0 + 1, :p] + pbias[:, o : o + p]
+            for c0, nc, at in rows.vector(PATCH + group, p):
+                part = pbias[:, o + c0 : o + c0 + nc]
+                acc[at : at + 1, side : side + nc] = acc[at : at + 1, side : side + nc] + part
 
         def pass_down(r):
             n = gn[r, :]
@@ -453,10 +468,13 @@
             dy[r, :] = dy[r, :] + a(r) * n
 
         over_rows(D, pass_down)
-        acc[rows.vec : rows.vec + 8, :] = acc[rows.vec : rows.vec + 8, :] + jnp.transpose(gcol[...])[:8]
+        sums = jnp.transpose(gcol[...])[:8]
+        for c0, nc, at in rows.vector(0, D):
+            acc[at : at + 8, side : side + nc] = acc[at : at + 8, side : side + nc] + sums[:, c0 : c0 + nc]
         for t in range(F // D):
-            r0 = rows.bias_in + t
-            acc[r0 : r0 + 1, :] = acc[r0 : r0 + 1, :] + gb1[0:1, t * D : (t + 1) * D]
+            for c0, nc, at in rows.vector(BIAS_IN + t, D):
+                part = gb1[0:1, t * D + c0 : t * D + c0 + nc]
+                acc[at : at + 1, side : side + nc] = acc[at : at + 1, side : side + nc] + part
         if final:
             half = rows.total // 2
             stages[l] = acc[pl.ds(pl.multiple_of((1 - core) * half, 16), half), :].astype(BF)
@@ -679,17 +697,24 @@
         if last:
             sources = [(layers - 1 - i, ref, 0) for i, ref in enumerate(misc_refs)] + [(0, full, rows.misc)]
             for l, ref, base in sources:
-                for j in range(7):
-                    at = rows.vec - rows.misc + base + j
-                    rest[j][l : l + 1, :] = ref[at : at + 1, :]
-                for t in range(ff // d):
-                    at = rows.bias_in - rows.misc + base + t
-                    rest[7][l : l + 1, t * d : (t + 1) * d] = ref[at : at + 1, :]
-                for g, p in enumerate(patches):
-                    at = rows.patch[g] - rows.misc + base
-                    rest[8 + g][l : l + 1, :] = ref[at : at + 1, :p]
-                    at, l0 = rows.mix[g][0] - rows.misc + base, rows.mix[g][1]
-                    rest[11 + g][:, l, :] = ref[at : at + p, l0 : l0 + p]
+                base -= rows.misc
+                side = rows.side
+                vectors = [(rest[j], 0, j, d) for j in range(7)]
+                vectors += [(rest[7], t * d, BIAS_IN + t, d) for t in range(ff // d)]
+                vectors += [(rest[8 + g], 0, PATCH + g, p) for g, p in enumerate(patches)]
+                for out, start, index, length in vectors:
+                    for c0, nc, at in rows.vector(index, length):
+                        out[l : l + 1, start + c0 : start + c0 + nc] = ref[base + at : base + at + 1, side : side + nc]
+                for g in range(len(patches)):
+                    parts = [
+                        (r0, ref[base + at : base + at + nr, lane : lane + nc])
+                        for r0, nr, _, nc, at, lane in rows.mix[g]
+                    ]
+                    whole = parts[0][1]
+                    if len(parts) > 1:
+                        low = jnp.concatenate([part for _, part in parts[1:]], 1)
+                        whole = jnp.concatenate([whole, low], 0)
+                    rest[11 + g][:, l, :] = whole
         else:
             rest[0][...] = full[rows.misc : rows.used, :]
         for cp in copies:

time: 278 us -> 277 us (level)
  waiting for transfers between devices: 32.9 us -> 26 us
  starting transfers between devices: 70.4 us -> 74.5 us
    ppermute x36, waiting for transfers between devices: 20.9 us -> 17.1 us  [cycle(): return lax.ppermute(v, 'swap', [(i, (i + s) % k) for i in range(k)])]
    ppermute x20, waiting for transfers between devices: 12 us -> 8.8 us  [flip(): return lax.ppermute(v, 'dp', [(i, i ^ bit) for i in range(n)])]
where the time goes in v1:
time: 277 us; the launch traced here: 273 us
  Pallas kernels  146 us (53%)
  starting transfers between devices  74.5 us (27%)
  waiting for transfers between devices  26 us (9%)
  local copies, waits for them, and re-layouts  24.9 us (9%)
    pallas_call x2, Pallas kernels, backward(): pl.pallas_call(functools.partial(backward_kernel, piece, k, patches, rows...  69.3 us
    ppermute x36, starting transfers between devices, cycle(): return lax.ppermute(v, 'swap', [(i, (i + s) % k) for i in range(k)])  46.4 us
    pallas_call x2, Pallas kernels, forward(): pl.pallas_call(functools.partial(forward_kernel, piece, k, patches, L), o...  38.7 us
    ppermute x20, starting transfers between devices, flip(): return lax.ppermute(v, 'dp', [(i, i ^ bit) for i in range(n)])  28 us
    unnamed x121, local copies, waits for them, and re-layouts  24.9 us
    ppermute x36, waiting for transfers between devices, cycle(): return lax.ppermute(v, 'swap', [(i, (i + s) % k) for i in range(k)])  17.1 us
    pallas_call x4, Pallas kernels, unpack(): pl.pallas_call(functools.partial(unpack_kernel, pieces, groups, k, patche...  11.5 us
    ppermute x20, waiting for transfers between devices, flip(): return lax.ppermute(v, 'dp', [(i, i ^ bit) for i in range(n)])  8.8 us
  transfers between devices with their start and end apart: 56, of which 12 were waited for; matrix products, arithmetic and copies ran while one was open for 2% of the time, Pallas kernels for 50%

profile of v1, /device:TPU:1, one launch (start us, length us, event | category | flops | bytes accessed | tf_op | source)
XLA Modules:
  0.0 273.1 jit_solution(7962582789548681813)
XLA Ops:
  4.5 2.2 collective-permute-start
  6.7 2.3 collective-permute-start.1
  13.2 1.9 copy.49.refs_8_.refs_22_
  24.9 4.9 %collective-permute-start.3 = (bf16[96,1280]{1,0:T(8,128)(2,1)}, bf16[96,1280]{1,0:T(8,128)(2,1)}, u32[]{:S(2)}, u32[]{:S(2)}) collective-permute-start(bf16[96,1280]{1,0:T(8,128)(2,1)} %get-tuple-element.268), channel_id=1, source_target_pairs={{0,1},{1,2},{2,3},{3,0},{4,5},{5,6},{6,7},{7,4},{8,9},{9,10},{10,1... | collective-permute-start | bytes 737288 | tf_op jit(solution)/shard_map/ppermute | solution.py:550
  30.2 1.9 collective-permute-start.5
  32.1 18.8 %forward.2 = (bf16[96,1152]{1,0:T(8,128)(2,1)}, bf16[96,1152]{1,0:T(8,128)(2,1)}, bf16[96,1152]{1,0:T(8,128)(2,1)}, bf16[96,1152]{1,0:T(8,128)(2,1)}, bf16[384,1...) custom-call(s32[2]{0:T(128)} %copy-done.10, ...), custom_call_target="tpu_custom_call" | custom-call | tf_op jit(solution)/shard_map/forward/pallas_call | solution.py:320
  50.9 1.8 collective-permute-start.6
  54.8 19.9 %forward.3 = (bf16[96,1280]{1,0:T(8,128)(2,1)}, bf16[96,1280]{1,0:T(8,128)(2,1)}, bf16[96,1280]{1,0:T(8,128)(2,1)}, bf16[96,1280]{1,0:T(8,128)(2,1)}, bf16[384,1...) custom-call(s32[2]{0:T(128)} %copy-done.10, ...), custom_call_target="tpu_custom_call" | custom-call | tf_op jit(solution)/shard_map/forward/pallas_call | solution.py:320
  78.4 3.0 %collective-permute-start.13 = (bf16[96,1152]{1,0:T(8,128)(2,1)}, bf16[96,1152]{1,0:T(8,128)(2,1)}, u32[]{:S(2)}, u32[]{:S(2)}) collective-permute-start(bf16[96,1152]{1,0:T(8,128)(2,1)} %get-tuple-element.296), channel_id=1, source_target_pairs={{0,3},{1,0},{2,1},{3,2},{4,7},{5,4},{6,5},{7,6},{8,11},{9,8},{10,9... | collective-permute-start | bytes 663560 | tf_op jit(solution)/shard_map/ppermute | solution.py:550
  81.4 32.9 %backward.2 = (bf16[96,1152]{1,0:T(8,128)(2,1)}, bf16[96,1152]{1,0:T(8,128)(2,1)}, bf16[96,1152]{1,0:T(8,128)(2,1)}, bf16[96,1152]{1,0:T(8,128)(2,1)}, f32[3584,384]{1,0:T(8,128)}, /*index=5*/f32[3584,384]{1,0:T(8,128)}) custom-call(s32[2]{0:T(128)} %copy-done.10, bf16[96,1152]{1,0:T(8,128)(2,1)} %copy-done.25, ...), custom_call_target="tpu_custom_call" | custom-call | tf_op jit(solution)/shard_map/backward/pallas_call | solution.py:527
  114.7 3.0 %collective-permute-start.17 = (bf16[96,1280]{1,0:T(8,128)(2,1)}, bf16[96,1280]{1,0:T(8,128)(2,1)}, u32[]{:S(2)}, u32[]{:S(2)}) collective-permute-start(bf16[96,1280]{1,0:T(8,128)(2,1)} %get-tuple-element.326), channel_id=1, source_target_pairs={{0,3},{1,0},{2,1},{3,2},{4,7},{5,4},{6,5},{7,6},{8,11},{9,8},{10,9... | collective-permute-start | bytes 737288 | tf_op jit(solution)/shard_map/ppermute | solution.py:550
  119.1 36.4 %backward.3 = (bf16[96,1280]{1,0:T(8,128)(2,1)}, bf16[96,1280]{1,0:T(8,128)(2,1)}, bf16[96,1280]{1,0:T(8,128)(2,1)}, bf16[96,1280]{1,0:T(8,128)(2,1)}, bf16[1792...) custom-call(s32[2]{0:T(128)} %copy-done.10, ...), custom_call_target="tpu_custom_call" | custom-call | tf_op jit(solution)/shard_map/backward/pallas_call | solution.py:527
  155.6 4.5 %collective-permute-start.18 = (bf16[1792,384]{1,0:T(8,128)(2,1)}, bf16[1792,384]{1,0:T(8,128)(2,1)S(1)}, u32[]{:S(2)}, u32[]{:S(2)}) collective-permute-start(bf16[1792,384]{1,0:T(8,128)(2,1)} %get-tuple-element.360), channel_id=1, source_target_pairs={{0,4},{4,0},{8,12},{12,8},{16,20},{20,16},{24,28},{28,24},{1,5},{5... | collective-permute-start | bytes 4128776 | tf_op jit(solution)/shard_map/ppermute | solution.py:546
  160.2 2.9 %collective-permute-done.18 = bf16[1792,384]{1,0:T(8,128)(2,1)S(1)} collective-permute-done((bf16[1792,384]{1,0:T(8,128)(2,1)}, bf16[1792,384]{1,0:T(8,128)(2,1)S(1)}, u32[]{:S(2)}, u32[]{:S(2)}) %collective-permute-start.18) | collective-permute-done | bytes 1376288 | tf_op jit(solution)/shard_map/ppermute | solution.py:546
  170.8 4.8 %collective-permute-done.23.refs_3_ = bf16[96,1152]{1,0:T(8,128)(2,1)S(1)} collective-permute-done((bf16[96,1152]{1,0:T(8,128)(2,1)S(1)}, bf16[96,1152]{1,0:T(8,128)(2,1)S(1)}, u32[]{:S(2)}, u32[]{:S(2)}) %collective-permute-start.23) | collective-permute-done | bytes 221216 | tf_op jit(solution)/shard_map/ppermute | solution.py:550
  180.9 2.2 collective-permute-done.26.c0
  189.1 2.0 split_swap.2
  195.1 2.0 split_swap.3
  198.7 2.3 collective-permute-start.39
  205.0 2.5 unpack.4
  208.4 7.4 %collective-permute-done.35.refs_2_ = bf16[112,384]{1,0:T(8,128)(2,1)S(1)} collective-permute-done((bf16[112,384]{1,0:T(8,128)(2,1)S(1)}, bf16[112,384]{1,0:T(8,128)(2,1)S(1)}, u32[]{:S(2)}, u32[]{:S(2)}) %collective-permute-start.35) | collective-permute-done | bytes 86048 | tf_op jit(solution)/shard_map/ppermute | solution.py:550
  217.1 1.8 join_swap.2
  225.1 4.4 %unpack.5 = (f32[24,96,100]{2,1,0:T(8,128)}, f32[24,96,196]{2,1,0:T(8,128)}) custom-call(s32[2]{0:T(128)S(1)} %copy-done.13, s32[3]{0:T(128)S(1)} %bitcast.46, bf16[96,1152]{1,0:T(8,128)(2,1)S(1)} %copy-done.7, bf16[96,1152]{1,0:T(8,128)(2,1)} %collective-permute-done.12.refs_1_, bf16[96,1152]{1,0:T(8,128)(2,1)} %collective-permute-done.14.refs_2_, ...), custom_call_target="tpu_custom_call" | custom-call | tf_op jit(solution)/shard_map/unpack/pallas_call | solution.py:102
  230.2 1.8 join_swap.3
  232.0 3.4 %collective-permute-start.47 = (bf16[96,1280]{1,0:T(8,128)(2,1)S(1)}, bf16[96,1280]{1,0:T(8,128)(2,1)S(1)}, u32[]{:S(2)}, u32[]{:S(2)}) collective-permute-start(bf16[96,1280]{1,0:T(8,128)(2,1)S(1)} %copy-done.55), channel_id=1, source_target_pairs={{0,3},{1,0},{2,1},{3,2},{4,7},{5,4},{6,5},{7,6},{8,11},{9,8},{10,9... | collective-permute-start | bytes 737288 | tf_op jit(solution)/shard_map/ppermute | solution.py:550
  237.7 2.5 collective-permute-done.48.c0
  248.9 7.7 %collective-permute-start.55 = (bf16[1792,384]{1,0:T(8,128)(2,1)S(1)}, bf16[1792,384]{1,0:T(8,128)(2,1)S(1)}, u32[]{:S(2)}, u32[]{:S(2)}) collective-permute-start(bf16[1792,384]{1,0:T(8,128)(2,1)S(1)} %bitcast.26), channel_id=1, source_target_pairs={{0,4},{4,0},{8,12},{12,8},{16,20},{20,16},{24,28},{28,24},{1,5},{5... | collective-permute-start | bytes 4128776 | tf_op jit(solution)/shard_map/ppermute | solution.py:546
  256.6 2.1 collective-permute-done.46.refs_6_
  259.4 2.7 %collective-permute-start.54 = (bf16[1792,384]{1,0:T(8,128)(2,1)S(1)}, bf16[1792,384]{1,0:T(8,128)(2,1)S(1)}, u32[]{:S(2)}, u32[]{:S(2)}) collective-permute-start(bf16[1792,384]{1,0:T(8,128)(2,1)S(1)} %bitcast.24), channel_id=1, source_target_pairs={{0,4},{4,0},{8,12},{12,8},{16,20},{20,16},{24,28},{28,24},{1,5},{5... | collective-permute-start | bytes 4128776 | tf_op jit(solution)/shard_map/ppermute | solution.py:546
  262.1 3.0 %unpack.7 = (f32[24,96,100]{2,1,0:T(8,128)}, f32[24,96,196]{2,1,0:T(8,128)}) custom-call(s32[2]{0:T(128)S(1)} %copy-done.14, s32[3]{0:T(128)S(1)} %bitcast.47, bf16[96,1152]{1,0:T(8,128)(2,1)S(1)} %copy-done.6, bf16[96,1152]{1,0:T(8,128)(2,1)S(1)} %collective-permute-done.22.refs_1_, bf16[96,1152]{1,0:T(8,128)(2,1)S(1)} %collective-permute-done.28.refs_2_, ...), custom_call_target="tpu_custom_call" | custom-call | tf_op jit(solution)/shard_map/unpack/pallas_call | solution.py:102
  265.1 3.3 %finish.2 = (f32[2,384,1536]{2,1,0:T(8,128)}, f32[2,1536,384]{2,1,0:T(8,128)}, f32[512,384]{1,0:T(8,128)S(1)}) custom-call(s32[2]{0:T(128)S(1)} %copy-done.14, bf16[1792,384]{1,0:T(8,128)(2,1)S(1)} %bitcast.27, bf16[1792,384]{1,0:T(8,128)(2,1)S(1)} %collective-permute-done.55.b_ref), custom_call_target="tpu_custom_call" | custom-call | tf_op jit(solution)/shard_map/finish/pallas_call | solution.py:726
  268.4 4.5 %finish.3 = (f32[2,384,1536]{2,1,0:T(8,128)}, f32[2,1536,384]{2,1,0:T(8,128)}, f32[2,384]{1,0:T(2,128)}, f32[2,384]{1,0:T(2,128)}, f32[2,384]{1,0:T(2,128)}, /*i...) custom-call(s32[2]{0:T(128)S(1)} %copy-done.14, ...), custom_call_target="tpu_custom_call", output_to_operand_aliasing={{0}: (3, {}), {1}: (4, {})} | custom-call | tf_op jit(solution)/shard_map/finish/pallas_call | solution.py:726
  (230 shorter events, 74.8 us)
Async XLA Ops:
  4.5 19.0 %collective-permute-start = (bf16[96,1152]{1,0:T(8,128)(2,1)S(1)}, bf16[96,1152]{1,0:T(8,128)(2,1)S(1)}, u32[]{:S(2)}, u32[]{:S(2)}) collective-permute-start(bf16[96,1152]{1,0:T(8,128)(2,1)S(1)} %get-tuple-element.260), channel_id=1, source_target_pairs={{0,1},{1,2},{2,3},{3,0},{4,5},{5,6},{6,7},{7,4},{8,9},{9,10},{10,1... | collective-permute-start | bytes 663560 | tf_op jit(solution)/shard_map/ppermute | solution.py:550
  6.7 17.4 %collective-permute-start.1 = (bf16[96,1152]{1,0:T(8,128)(2,1)S(1)}, bf16[96,1152]{1,0:T(8,128)(2,1)S(1)}, u32[]{:S(2)}, u32[]{:S(2)}) collective-permute-start(bf16[96,1152]{1,0:T(8,128)(2,1)S(1)} %get-tuple-element.261), channel_id=1, source_target_pairs={{0,2},{1,3},{2,0},{3,1},{4,6},{5,7},{6,4},{7,5},{8,10},{9,11},{10,... | collective-permute-start | bytes 663560 | tf_op jit(solution)/shard_map/ppermute | solution.py:550
  9.0 15.1 %collective-permute-start.2 = (bf16[96,1152]{1,0:T(8,128)(2,1)S(1)}, bf16[96,1152]{1,0:T(8,128)(2,1)S(1)}, u32[]{:S(2)}, u32[]{:S(2)}) collective-permute-start(bf16[96,1152]{1,0:T(8,128)(2,1)S(1)} %get-tuple-element.262), channel_id=1, source_target_pairs={{0,3},{1,0},{2,1},{3,2},{4,7},{5,4},{6,5},{7,6},{8,11},{9,8},{10,9... | collective-permute-start | bytes 663560 | tf_op jit(solution)/shard_map/ppermute | solution.py:550
  24.9 26.0 %collective-permute-start.3 = (bf16[96,1280]{1,0:T(8,128)(2,1)}, bf16[96,1280]{1,0:T(8,128)(2,1)}, u32[]{:S(2)}, u32[]{:S(2)}) collective-permute-start(bf16[96,1280]{1,0:T(8,128)(2,1)} %get-tuple-element.268), channel_id=1, source_target_pairs={{0,1},{1,2},{2,3},{3,0},{4,5},{5,6},{6,7},{7,4},{8,9},{9,10},{10,1... | collective-permute-start | bytes 737288 | tf_op jit(solution)/shard_map/ppermute | solution.py:550
  29.9 21.1 %collective-permute-start.4 = (bf16[96,1280]{1,0:T(8,128)(2,1)}, bf16[96,1280]{1,0:T(8,128)(2,1)}, u32[]{:S(2)}, u32[]{:S(2)}) collective-permute-start(bf16[96,1280]{1,0:T(8,128)(2,1)} %get-tuple-element.269), channel_id=1, source_target_pairs={{0,2},{1,3},{2,0},{3,1},{4,6},{5,7},{6,4},{7,5},{8,10},{9,11},{10,... | collective-permute-start | bytes 737288 | tf_op jit(solution)/shard_map/ppermute | solution.py:550
  30.2 20.8 %collective-permute-start.5 = (bf16[96,1280]{1,0:T(8,128)(2,1)}, bf16[96,1280]{1,0:T(8,128)(2,1)}, u32[]{:S(2)}, u32[]{:S(2)}) collective-permute-start(bf16[96,1280]{1,0:T(8,128)(2,1)} %get-tuple-element.270), channel_id=1, source_target_pairs={{0,3},{1,0},{2,1},{3,2},{4,7},{5,4},{6,5},{7,6},{8,11},{9,8},{10,9... | collective-permute-start | bytes 737288 | tf_op jit(solution)/shard_map/ppermute | solution.py:550
  50.9 23.8 %collective-permute-start.6 = (bf16[96,1152]{1,0:T(8,128)(2,1)}, bf16[96,1152]{1,0:T(8,128)(2,1)}, u32[]{:S(2)}, u32[]{:S(2)}) collective-permute-start(bf16[96,1152]{1,0:T(8,128)(2,1)} %copy-done.40), channel_id=1, source_target_pairs={{0,1},{1,2},{2,3},{3,0},{4,5},{5,6},{6,7},{7,4},{8,9},{9,10},{10,1... | collective-permute-start | bytes 663560 | tf_op jit(solution)/shard_map/ppermute | solution.py:550
  52.7 22.0 %collective-permute-start.7 = (bf16[96,1152]{1,0:T(8,128)(2,1)}, bf16[96,1152]{1,0:T(8,128)(2,1)}, u32[]{:S(2)}, u32[]{:S(2)}) collective-permute-start(bf16[96,1152]{1,0:T(8,128)(2,1)} %copy-done.39), channel_id=1, source_target_pairs={{0,2},{1,3},{2,0},{3,1},{4,6},{5,7},{6,4},{7,5},{8,10},{9,11},{10,... | collective-permute-start | bytes 663560 | tf_op jit(solution)/shard_map/ppermute | solution.py:550
  54.2 20.5 %collective-permute-start.8 = (bf16[96,1152]{1,0:T(8,128)(2,1)}, bf16[96,1152]{1,0:T(8,128)(2,1)}, u32[]{:S(2)}, u32[]{:S(2)}) collective-permute-start(bf16[96,1152]{1,0:T(8,128)(2,1)} %copy-done.38), channel_id=1, source_target_pairs={{0,3},{1,0},{2,1},{3,2},{4,7},{5,4},{6,5},{7,6},{8,11},{9,8},{10,9... | collective-permute-start | bytes 663560 | tf_op jit(solution)/shard_map/ppermute | solution.py:550
  74.8 39.6 %collective-permute-start.9 = (bf16[96,1280]{1,0:T(8,128)(2,1)}, bf16[96,1280]{1,0:T(8,128)(2,1)}, u32[]{:S(2)}, u32[]{:S(2)}) collective-permute-start(bf16[96,1280]{1,0:T(8,128)(2,1)} %copy-done.37), channel_id=1, source_target_pairs={{0,1},{1,2},{2,3},{3,0},{4,5},{5,6},{6,7},{7,4},{8,9},{9,10},{10,1... | collective-permute-start | bytes 737288 | tf_op jit(solution)/shard_map/ppermute | solution.py:550
  75.7 38.6 %collective-permute-start.10 = (bf16[96,1280]{1,0:T(8,128)(2,1)}, bf16[96,1280]{1,0:T(8,128)(2,1)}, u32[]{:S(2)}, u32[]{:S(2)}) collective-permute-start(bf16[96,1280]{1,0:T(8,128)(2,1)} %copy-done.36), channel_id=1, source_target_pairs={{0,2},{1,3},{2,0},{3,1},{4,6},{5,7},{6,4},{7,5},{8,10},{9,11},{10,... | collective-permute-start | bytes 737288 | tf_op jit(solution)/shard_map/ppermute | solution.py:550
  76.6 37.8 %collective-permute-start.11 = (bf16[96,1280]{1,0:T(8,128)(2,1)}, bf16[96,1280]{1,0:T(8,128)(2,1)}, u32[]{:S(2)}, u32[]{:S(2)}) collective-permute-start(bf16[96,1280]{1,0:T(8,128)(2,1)} %copy-done.35), channel_id=1, source_target_pairs={{0,3},{1,0},{2,1},{3,2},{4,7},{5,4},{6,5},{7,6},{8,11},{9,8},{10,9... | collective-permute-start | bytes 737288 | tf_op jit(solution)/shard_map/ppermute | solution.py:550
  78.1 36.2 %collective-permute-start.12 = (bf16[96,1152]{1,0:T(8,128)(2,1)}, bf16[96,1152]{1,0:T(8,128)(2,1)}, u32[]{:S(2)}, u32[]{:S(2)}) collective-permute-start(bf16[96,1152]{1,0:T(8,128)(2,1)} %get-tuple-element.295), channel_id=1, source_target_pairs={{0,1},{1,2},{2,3},{3,0},{4,5},{5,6},{6,7},{7,4},{8,9},{9,10},{10,1... | collective-permute-start | bytes 663560 | tf_op jit(solution)/shard_map/ppermute | solution.py:550
  78.4 35.9 %collective-permute-start.13 = (bf16[96,1152]{1,0:T(8,128)(2,1)}, bf16[96,1152]{1,0:T(8,128)(2,1)}, u32[]{:S(2)}, u32[]{:S(2)}) collective-permute-start(bf16[96,1152]{1,0:T(8,128)(2,1)} %get-tuple-element.296), channel_id=1, source_target_pairs={{0,3},{1,0},{2,1},{3,2},{4,7},{5,4},{6,5},{7,6},{8,11},{9,8},{10,9... | collective-permute-start | bytes 663560 | tf_op jit(solution)/shard_map/ppermute | solution.py:550
  114.4 41.2 %collective-permute-start.15 = (bf16[96,1280]{1,0:T(8,128)(2,1)}, bf16[96,1280]{1,0:T(8,128)(2,1)}, u32[]{:S(2)}, u32[]{:S(2)}) collective-permute-start(bf16[96,1280]{1,0:T(8,128)(2,1)} %get-tuple-element.324), channel_id=1, source_target_pairs={{0,1},{1,2},{2,3},{3,0},{4,5},{5,6},{6,7},{7,4},{8,9},{9,10},{10,1... | collective-permute-start | bytes 737288 | tf_op jit(solution)/shard_map/ppermute | solution.py:550
  114.4 41.2 %collective-permute-start.16 = (bf16[96,1280]{1,0:T(8,128)(2,1)}, bf16[96,1280]{1,0:T(8,128)(2,1)}, u32[]{:S(2)}, u32[]{:S(2)}) collective-permute-start(bf16[96,1280]{1,0:T(8,128)(2,1)} %get-tuple-element.325), channel_id=1, source_target_pairs={{0,2},{1,3},{2,0},{3,1},{4,6},{5,7},{6,4},{7,5},{8,10},{9,11},{10,... | collective-permute-start | bytes 737288 | tf_op jit(solution)/shard_map/ppermute | solution.py:550
  114.7 40.9 %collective-permute-start.17 = (bf16[96,1280]{1,0:T(8,128)(2,1)}, bf16[96,1280]{1,0:T(8,128)(2,1)}, u32[]{:S(2)}, u32[]{:S(2)}) collective-permute-start(bf16[96,1280]{1,0:T(8,128)(2,1)} %get-tuple-element.326), channel_id=1, source_target_pairs={{0,3},{1,0},{2,1},{3,2},{4,7},{5,4},{6,5},{7,6},{8,11},{9,8},{10,9... | collective-permute-start | bytes 737288 | tf_op jit(solution)/shard_map/ppermute | solution.py:550
  117.7 37.9 %collective-permute-start.14 = (bf16[96,1152]{1,0:T(8,128)(2,1)}, bf16[96,1152]{1,0:T(8,128)(2,1)}, u32[]{:S(2)}, u32[]{:S(2)}) collective-permute-start(bf16[96,1152]{1,0:T(8,128)(2,1)} %get-tuple-element.321), channel_id=1, source_target_pairs={{0,2},{1,3},{2,0},{3,1},{4,6},{5,7},{6,4},{7,5},{8,10},{9,11},{10,... | collective-permute-start | bytes 663560 | tf_op jit(solution)/shard_map/ppermute | solution.py:550
  160.2 10.0 %collective-permute-start.22 = (bf16[96,1152]{1,0:T(8,128)(2,1)}, bf16[96,1152]{1,0:T(8,128)(2,1)S(1)}, u32[]{:S(2)}, u32[]{:S(2)}) collective-permute-start(bf16[96,1152]{1,0:T(8,128)(2,1)} %get-tuple-element.372), channel_id=1, source_target_pairs={{0,1},{1,2},{2,3},{3,0},{4,5},{5,6},{6,7},{7,4},{8,9},{9,10},{10,1... | collective-permute-start | bytes 663560 | tf_op jit(solution)/shard_map/ppermute | solution.py:550
  169.6 13.4 %collective-permute-start.26 = (bf16[4,112,384]{2,1,0:T(8,128)(2,1)S(1)}, bf16[4,112,384]{2,1,0:T(8,128)(2,1)S(1)}, u32[]{:S(2)}, u32[]{:S(2)}) collective-permute-start(bf16[4,112,384]{2,1,0:T(8,128)(2,1)S(1)} %get-tuple-element.369), channel_id=1, source_target_pairs={{0,8},{4,12},{8,0},{12,4},{16,24},{20,28},{24,16},{28,20},{1,9},{5... | collective-permute-start | bytes 1032200 | tf_op jit(solution)/shard_map/ppermute | solution.py:546
  170.0 14.0 %collective-permute-start.27 = (bf16[4,112,384]{2,1,0:T(8,128)(2,1)S(1)}, bf16[4,112,384]{2,1,0:T(8,128)(2,1)S(1)}, u32[]{:S(2)}, u32[]{:S(2)}) collective-permute-start(bf16[4,112,384]{2,1,0:T(8,128)(2,1)S(1)} %get-tuple-element.371), channel_id=1, source_target_pairs={{0,16},{4,20},{8,24},{12,28},{16,0},{20,4},{24,8},{28,12},{1,17},{... | collective-permute-start | bytes 1032200 | tf_op jit(solution)/shard_map/ppermute | solution.py:546
  175.6 12.7 %collective-permute-start.28 = (bf16[96,1152]{1,0:T(8,128)(2,1)S(1)}, bf16[96,1152]{1,0:T(8,128)(2,1)S(1)}, u32[]{:S(2)}, u32[]{:S(2)}) collective-permute-start(bf16[96,1152]{1,0:T(8,128)(2,1)S(1)} %copy-done.57), channel_id=1, source_target_pairs={{0,2},{1,3},{2,0},{3,1},{4,6},{5,7},{6,4},{7,5},{8,10},{9,11},{10,... | collective-permute-start | bytes 663560 | tf_op jit(solution)/shard_map/ppermute | solution.py:550
  197.4 10.0 %collective-permute-start.38 = (bf16[112,384]{1,0:T(8,128)(2,1)}, bf16[112,384]{1,0:T(8,128)(2,1)S(1)}, u32[]{:S(2)}, u32[]{:S(2)}) collective-permute-start(bf16[112,384]{1,0:T(8,128)(2,1)} %get-tuple-element.398), channel_id=1, source_target_pairs={{0,2},{1,3},{2,0},{3,1},{4,6},{5,7},{6,4},{7,5},{8,10},{9,11},{10,... | collective-permute-start | bytes 258056 | tf_op jit(solution)/shard_map/ppermute | solution.py:550
  203.3 12.5 %collective-permute-start.35 = (bf16[112,384]{1,0:T(8,128)(2,1)S(1)}, bf16[112,384]{1,0:T(8,128)(2,1)S(1)}, u32[]{:S(2)}, u32[]{:S(2)}) collective-permute-start(bf16[112,384]{1,0:T(8,128)(2,1)S(1)} %add_swap.2.refs_0_), channel_id=1, source_target_pairs={{0,2},{1,3},{2,0},{3,1},{4,6},{5,7},{6,4},{7,5},{8,10},{9,11},{10,... | collective-permute-start | bytes 258056 | tf_op jit(solution)/shard_map/ppermute | solution.py:550
  203.9 11.9 %collective-permute-start.34 = (bf16[112,384]{1,0:T(8,128)(2,1)S(1)}, bf16[112,384]{1,0:T(8,128)(2,1)S(1)}, u32[]{:S(2)}, u32[]{:S(2)}) collective-permute-start(bf16[112,384]{1,0:T(8,128)(2,1)S(1)} %add_swap.2.refs_0_), channel_id=1, source_target_pairs={{0,1},{1,2},{2,3},{3,0},{4,5},{5,6},{6,7},{7,4},{8,9},{9,10},{10,1... | collective-permute-start | bytes 258056 | tf_op jit(solution)/shard_map/ppermute | solution.py:550
  218.9 10.7 %collective-permute-start.43 = (bf16[2,112,384]{2,1,0:T(8,128)(2,1)}, bf16[2,112,384]{2,1,0:T(8,128)(2,1)S(1)}, u32[]{:S(2)}, u32[]{:S(2)}) collective-permute-start(bf16[2,112,384]{2,1,0:T(8,128)(2,1)} %get-tuple-element.413.v0), channel_id=1, source_target_pairs={{0,16},{4,20},{8,24},{12,28},{16,0},{20,4},{24,8},{28,12},{1,17},{... | collective-permute-start | bytes 516104 | tf_op jit(solution)/shard_map/ppermute | solution.py:546
  219.4 10.1 %collective-permute-start.44 = (bf16[2,112,384]{2,1,0:T(8,128)(2,1)}, bf16[2,112,384]{2,1,0:T(8,128)(2,1)S(1)}, u32[]{:S(2)}, u32[]{:S(2)}) collective-permute-start(bf16[2,112,384]{2,1,0:T(8,128)(2,1)} %get-tuple-element.414.v1), channel_id=1, source_target_pairs={{0,8},{4,12},{8,0},{12,4},{16,24},{20,28},{24,16},{28,20},{1,9},{5... | collective-permute-start | bytes 516104 | tf_op jit(solution)/shard_map/ppermute | solution.py:546
  236.5 11.7 %collective-permute-start.52 = (bf16[4,112,384]{2,1,0:T(8,128)(2,1)S(1)}, bf16[4,112,384]{2,1,0:T(8,128)(2,1)S(1)}, u32[]{:S(2)}, u32[]{:S(2)}) collective-permute-start(bf16[4,112,384]{2,1,0:T(8,128)(2,1)S(1)} %get-tuple-element.435.v0), channel_id=1, source_target_pairs={{0,8},{4,12},{8,0},{12,4},{16,24},{20,28},{24,16},{28,20},{1,9},{5... | collective-permute-start | bytes 1032200 | tf_op jit(solution)/shard_map/ppermute | solution.py:546
  243.9 14.8 %collective-permute-start.50 = (bf16[4,112,384]{2,1,0:T(8,128)(2,1)S(1)}, bf16[4,112,384]{2,1,0:T(8,128)(2,1)S(1)}, u32[]{:S(2)}, u32[]{:S(2)}) collective-permute-start(bf16[4,112,384]{2,1,0:T(8,128)(2,1)S(1)} %get-tuple-element.439.v0), channel_id=1, source_target_pairs={{0,8},{4,12},{8,0},{12,4},{16,24},{20,28},{24,16},{28,20},{1,9},{5... | collective-permute-start | bytes 1032200 | tf_op jit(solution)/shard_map/ppermute | solution.py:546
  245.1 13.6 %collective-permute-start.51 = (bf16[4,112,384]{2,1,0:T(8,128)(2,1)S(1)}, bf16[4,112,384]{2,1,0:T(8,128)(2,1)S(1)}, u32[]{:S(2)}, u32[]{:S(2)}) collective-permute-start(bf16[4,112,384]{2,1,0:T(8,128)(2,1)S(1)} %get-tuple-element.440.v1), channel_id=1, source_target_pairs={{0,16},{4,20},{8,24},{12,28},{16,0},{20,4},{24,8},{28,12},{1,17},{... | collective-permute-start | bytes 1032200 | tf_op jit(solution)/shard_map/ppermute | solution.py:546
  246.8 11.9 %collective-permute-start.46 = (bf16[96,1280]{1,0:T(8,128)(2,1)S(1)}, bf16[96,1280]{1,0:T(8,128)(2,1)S(1)}, u32[]{:S(2)}, u32[]{:S(2)}) collective-permute-start(bf16[96,1280]{1,0:T(8,128)(2,1)S(1)} %copy-done.54), channel_id=1, source_target_pairs={{0,2},{1,3},{2,0},{3,1},{4,6},{5,7},{6,4},{7,5},{8,10},{9,11},{10,... | collective-permute-start | bytes 737288 | tf_op jit(solution)/shard_map/ppermute | solution.py:550
  248.9 16.2 %collective-permute-start.55 = (bf16[1792,384]{1,0:T(8,128)(2,1)S(1)}, bf16[1792,384]{1,0:T(8,128)(2,1)S(1)}, u32[]{:S(2)}, u32[]{:S(2)}) collective-permute-start(bf16[1792,384]{1,0:T(8,128)(2,1)S(1)} %bitcast.26), channel_id=1, source_target_pairs={{0,4},{4,0},{8,12},{12,8},{16,20},{20,16},{24,28},{28,24},{1,5},{5... | collective-permute-start | bytes 4128776 | tf_op jit(solution)/shard_map/ppermute | solution.py:546
  (83 other events, 701.1 us)
